TPU v7x, 256 devices: a whole 4x4x8 slice. The times are simulated.
256 devices in a mesh: ctx: 32 (over y, x, core), head: 8 (over z).
Axes of the slice: x: 4, y: 4, z: 8, core: 2. Of those that a mesh axis runs over, the one named last changes fastest.
Arguments:
- query_rows: bfloat16 [16384, 8192], P('ctx', 'head'), may hold values from -6 to 6
- key_rows: bfloat16 [16384, 8192], P('ctx', 'head'), may hold values from -6 to 6
- value_rows: bfloat16 [16384, 8192], P('ctx', 'head'), may hold values from -18 to 18
- out_grad: bfloat16 [16384, 8192], P('ctx', 'head'), may hold values from -6 to 6
- norm_gain: float32 [8192], P('head'), may hold values from 0.5 to 2
- doc_ids: int32 [16384], P('ctx'), may hold values from 0 to 31, never falling along the last dimension, each value on 1 to 8192 neighbouring positions
Outputs:
- normed_out: bfloat16 [16384, 8192], P('ctx', 'head')
- query_grad: bfloat16 [16384, 8192], P('ctx', 'head')
- key_grad: bfloat16 [16384, 8192], P('ctx', 'head')
- value_grad: bfloat16 [16384, 8192], P('ctx', 'head')
All inputs are finite; a program needn't handle non-finite values.
Results may differ from a plain program's by a relative error of at most 0.006.
Values sent between devices are 32-bit elements; how exact they have to be, the bound alone decides.
A program may use at most 128 MiB of HBM per device.

v0:
```python
import jax
import jax.numpy as jnp
from jax import lax
from jax.sharding import PartitionSpec as P

DH = 128


epsilon = 1e-05


def carried_in(shard, axis, combine, identity):
    peers, position = (lax.axis_size(axis), lax.axis_index(axis))
    everything = jax.tree.map(lambda part: lax.all_gather(part, axis), shard)
    start = jax.tree.map(
        lambda part, zero: jnp.broadcast_to(jnp.asarray(zero, part.dtype), part.shape),
        shard,
        identity,
    )

    def turn(k, before):
        at = peers - 1 - k
        reached = at > position
        new = combine(before, jax.tree.map(lambda part: part[at], everything))
        return jax.tree.map(lambda a, b: jnp.where(reached, a, b), new, before)

    return lax.fori_loop(0, peers, turn, start)


def join_backward(earlier, later):
    high_state, high_first, high_last = earlier
    low_state, low_first, low_last = later
    low_empty = low_first < 0
    joined = (low_first == low_last) & (low_last == high_first)
    state = jnp.where(low_empty, high_state, low_state + jnp.where(joined, high_state, 0.0))
    first_id = jnp.where(low_empty, high_first, low_first)
    last_id = jnp.where(high_first < 0, low_last, high_last)
    return (state, first_id, last_id)


def body(query_rows, key_rows, value_rows, out_grad, norm_gain, doc_ids):
    tokens_here = query_rows.shape[0]
    heads_here = norm_gain.shape[0] // DH
    block_shape = (tokens_here, heads_here, DH)
    queries = query_rows.reshape(block_shape)
    keyset = key_rows.reshape(block_shape)
    values = value_rows.reshape(block_shape)
    gain_heads = norm_gain.reshape(heads_here, DH)
    first_id = doc_ids[0]
    last_id = doc_ids[-1]
    positions = jnp.arange(tokens_here)
    same_doc = (doc_ids[:, None] == doc_ids[None, :]) & (positions[:, None] >= positions[None, :])
    first_float = (doc_ids == first_id).astype(jnp.float32)[:, None, None]
    last_float = (doc_ids == last_id).astype(jnp.float32)[:, None, None]
    first_half = (doc_ids == first_id).astype(jnp.bfloat16)[:, None, None]
    last_half = (doc_ids == last_id).astype(jnp.bfloat16)[:, None, None]
    zero_state = jnp.zeros((heads_here, DH, DH), jnp.float32)
    no_doc = jnp.int32(-1)
    raw_scores = jnp.einsum("thd,shd->hts", queries, keyset, preferred_element_type=jnp.float32)
    weights = jnp.where(same_doc[None], raw_scores, 0.0).astype(jnp.bfloat16)
    piece = jnp.einsum(
        "shd,she->hde", keyset * last_half, values, preferred_element_type=jnp.float32
    )
    device = lax.axis_index("ctx")
    states = lax.all_gather(piece[None], "ctx", axis=0, tiled=True)
    lasts = lax.all_gather(jnp.reshape(last_id, (1,)), "ctx", axis=0, tiled=True)
    sources = jnp.arange(lasts.shape[0])
    keep = (lasts == first_id) & (sources < device)
    incoming = jnp.sum(jnp.where(keep[:, None, None, None], states, 0.0), axis=0)
    state_in = incoming.astype(jnp.bfloat16)
    attended = jnp.einsum("hts,shd->thd", weights, values, preferred_element_type=jnp.float32)
    attended = (
        attended
        + jnp.einsum("thd,hde->the", queries, state_in, preferred_element_type=jnp.float32)
        * first_float
    )
    scaled = gain_heads * out_grad.reshape(block_shape).astype(jnp.float32)
    square_sums, grad_sums = lax.psum(
        (jnp.sum(attended * attended, axis=(1, 2)), jnp.sum(scaled * attended, axis=(1, 2))), "head"
    )
    width = heads_here * DH * lax.axis_size("head")
    inv_rms = lax.rsqrt(square_sums / width + epsilon)[:, None, None]
    normed = (gain_heads * attended * inv_rms).astype(jnp.bfloat16)
    stat = (grad_sums / width)[:, None, None]
    out_adj = (inv_rms * scaled - attended * inv_rms * inv_rms * inv_rms * stat).astype(
        jnp.bfloat16
    )
    adj_scores = jnp.einsum("thd,shd->hts", out_adj, values, preferred_element_type=jnp.float32)
    adj_weights = jnp.where(same_doc[None], adj_scores, 0.0).astype(jnp.bfloat16)
    query_grad = jnp.einsum("hts,shd->thd", adj_weights, keyset, preferred_element_type=jnp.float32)
    query_grad = (
        query_grad
        + jnp.einsum("the,hde->thd", out_adj, state_in, preferred_element_type=jnp.float32)
        * first_float
    )
    back_piece = jnp.einsum(
        "thd,the->hde", out_adj * first_half, queries, preferred_element_type=jnp.float32
    )
    suffix_state, suffix_first, suffix_last = carried_in(
        (back_piece, first_id, last_id), "ctx", join_backward, (zero_state, no_doc, no_doc)
    )
    outgoing = jnp.where(suffix_first == last_id, suffix_state, 0.0)
    state_back = outgoing.astype(jnp.bfloat16)
    key_grad = jnp.einsum("hts,thd->shd", adj_weights, queries, preferred_element_type=jnp.float32)
    key_grad = (
        key_grad
        + jnp.einsum("shd,hde->she", values, state_back, preferred_element_type=jnp.float32)
        * last_float
    )
    value_grad = jnp.einsum("hts,thd->shd", weights, out_adj, preferred_element_type=jnp.float32)
    value_grad = (
        value_grad
        + jnp.einsum("she,hde->shd", keyset, state_back, preferred_element_type=jnp.float32)
        * last_float
    )
    flat = (tokens_here, heads_here * DH)
    return (
        normed.reshape(flat),
        query_grad.astype(jnp.bfloat16).reshape(flat),
        key_grad.astype(jnp.bfloat16).reshape(flat),
        value_grad.astype(jnp.bfloat16).reshape(flat),
    )


def solution(mesh):
    placed = (
        P("ctx", "head"),
        P("ctx", "head"),
        P("ctx", "head"),
        P("ctx", "head"),
        P("head"),
        P("ctx"),
    )
    return jax.shard_map(
        body,
        mesh=mesh,
        in_specs=placed,
        out_specs=(P("ctx", "head"), P("ctx", "head"), P("ctx", "head"), P("ctx", "head")),
        check_vma=False,
    )
```

profile of v0, /device:TPU:1, one launch (start us, length us, event | category | flops | bytes accessed | tf_op | source)
XLA Modules:
  0.0 413.7 jit_solution(11023165825794695964)
XLA Ops:
  7.2 1.3 dynamic-slice
  8.6 2.0 fusion.38
  10.6 1.9 fusion.37
  12.5 1.5 copy.59
  16.1 1.5 copy.38
  18.4 14.5 %all-reduce.2 = (s32[32]{0:T(128)S(1)}, s32[32]{0:T(128)S(1)}) all-reduce(s32[32]{0:T(128)S(1)} %get-tuple-element.244, s32[32]{0:T(128)S(1)} %slice_dynamic-update-slice_fusion), channel_id=1, replica_groups=mesh['ctx'=32,'head'=8] {'ctx'}, use_global_device_ids=true, to_apply=%add | all-reduce | flops 64 | bytes 512
  34.4 4.8 %select_convert_fusion.1 = bf16[8,512,512]{2,1,0:T(8,128)(2,1)} fusion(pred[512,512]{1,0:T(8,128)(4,1)S(1)} %fusion.18, bf16[512,1024]{1,0:T(8,128)(2,1)} %param.9, bf16[512,1024]{1,0:T(8,128)(2,1)} %param.8), kind=kOutput, calls=%fused_computation.4 | convolution fusion | flops 541065216 | bytes 6553600 | tf_op jit(solution)/shard_map/thd,shd->hts/dot_general | solution.py:59
  39.2 58.7 %all-gather.5.cloned.1.call-done = f32[256,128,128]{2,1,0:T(8,128)} async-done(((f32[8,128,128]{2,1,0:T(8,128)}), f32[256,128,128]{2,1,0:T(8,128)}) %all-gather.5.cloned.1.call-update) | async-done | bytes 16777232 | tf_op jit(solution)/shard_map/all_gather | solution.py:65
  97.9 7.8 %select_reduce_fusion = bf16[8,128,128]{2,1,0:T(8,128)(2,1)S(1)} fusion(f32[32,8,128,128]{3,2,1,0:T(8,128)} %bitcast.113, pred[32]{0:T(512)(128)(4,1)S(1)} %compare_and_fusion), kind=kLoop, calls=%fused_computation.2 | loop fusion | flops 8257536 | bytes 17039392 | tf_op jit(solution)/shard_map/reduce_sum | solution.py:69
  106.4 5.2 %multiply_reduce_fusion = (f32[512]{0:T(512)S(1)}, f32[512]{0:T(512)S(1)}, f32[512,8,128]{0,2,1:T(8,128)}) fusion(f32[512,1024]{0,1:T(8,128)S(1)} %copy.38, f32[8,128]{1,0:T(8,128)S(1)} %bitcast.121, f32[8,128,512]{2,1,0:T(8,128)S(1)} %fusion.14, f32[512]{0:T(512)S(1)} %convert_element_type.51, bf16[8,512,512]{2,1,0:T(8,128)(2,1)} %select_convert_fusion.1, ...), kind=kOutput, calls=%fused_computation.12 | convolution fusion | flops 540539904 | bytes 11544576 | tf_op jit(solution)/shard_map/hts,shd->thd/dot_general | solution.py:71
  111.6 14.0 %all-reduce.3 = (f32[512]{0:T(512)S(1)}, f32[512]{0:T(512)S(1)}) all-reduce(f32[512]{0:T(512)S(1)} %get-tuple-element.216, f32[512]{0:T(512)S(1)} %get-tuple-element.215), channel_id=1, replica_groups=mesh['ctx'=32,'head'=8] {'head'}, use_global_device_ids=true, to_apply=%region_2.3 | all-reduce | flops 1024 | bytes 8192 | tf_op jit(solution)/shard_map/psum | solution.py:78
  125.6 3.4 subtract_convert_fusion
  131.3 2.4 copy.48
  134.6 1.4 select_convert_fusion
  136.0 2.5 fusion.1
  138.5 2.3 copy.49
  140.7 4.3 %fusion.39 = f32[8,128,512]{2,1,0:T(8,128)} fusion(bf16[512,8,128]{0,2,1:T(8,128)(2,1)S(1)} %copy-done.3, bf16[8,512,512]{2,1,0:T(8,128)(2,1)} %select_convert_fusion.1), kind=kOutput, calls=%fused_computation.61 | convolution fusion | flops 536870912 | bytes 7340032 | tf_op jit(solution)/shard_map/hts,thd->shd/dot_general | solution.py:110
  145.0 64.4 %all-gather.7.cloned.1.call-done = f32[256,128,128]{2,1,0:T(8,128)} async-done(((f32[8,128,128]{2,1,0:T(8,128)}), f32[256,128,128]{2,1,0:T(8,128)}) %all-gather.7.cloned.1.call-update) | async-done | bytes 16777232 | tf_op jit(solution)/shard_map/all_gather | solution.py:14
  209.4 184.4 %while.18 = (s32[]{:T(128)}, f32[8,128,128]{2,1,0:T(8,128)S(1)}, s32[]{:T(128)}, s32[]{:T(128)}, s32[32]{0:T(128)S(1)}, /*index=5*/f32[32,8,128,128]{3,2,1,0:T(8...) while((s32[]{:T(128)}, f32[8,128,128]{2,1,0:T(8,128)S(1)}, ...), condition=%wide.region_6.7_spmd.clone, body=%wide.region_5.6_spmd.clone.sunk | while | flops 655374 | bytes 1573141 | solution.py:27
  213.8 1.3 select_select_fusion.2
  219.6 1.3 select_select_fusion.2
  225.4 1.3 select_select_fusion.2
  231.1 1.3 select_select_fusion.2
  236.9 1.3 select_select_fusion.2
  242.7 1.3 select_select_fusion.2
  248.4 1.3 select_select_fusion.2
  254.2 1.3 select_select_fusion.2
  259.9 1.3 select_select_fusion.2
  265.7 1.3 select_select_fusion.2
  271.5 1.3 select_select_fusion.2
  277.2 1.3 select_select_fusion.2
  283.0 1.3 select_select_fusion.2
  288.7 1.3 select_select_fusion.2
  294.5 1.3 select_select_fusion.2
  300.3 1.3 select_select_fusion.2
  306.0 1.3 select_select_fusion.2
  311.8 1.3 select_select_fusion.2
  317.6 1.3 select_select_fusion.2
  323.3 1.3 select_select_fusion.2
  329.1 1.3 select_select_fusion.2
  334.8 1.3 select_select_fusion.2
  357.9 1.3 select_select_fusion.2
  375.2 1.3 select_select_fusion.2
  394.5 1.8 fusion.3
  396.4 1.5 add_convert_fusion
  397.9 2.4 copy.51
  400.3 4.3 %fusion = bf16[512,8,128]{0,2,1:T(8,128)(2,1)} fusion(f32[8,128,512]{2,1,0:T(8,128)S(1)} %copy-done.5, bf16[8,512,512]{2,1,0:T(8,128)(2,1)} %copy-done.1, f32[512]{0:T(512)S(1)} %get-tuple-element.241, bf16[512,1024]{1,0:T(8,128)(2,1)} %param.8), kind=kOutput, calls=%fused_computation.6 | convolution fusion | flops 538443776 | bytes 8390656 | tf_op jit(solution)/shard_map/hts,thd->shd/dot_general | solution.py:104
  404.6 2.3 copy.50
  (120 shorter events, 56.4 us)
Async XLA Ops:
  7.2 7.6 %copy-start = (bf16[512,1024]{1,0:T(8,128)(2,1)S(1)}, bf16[512,1024]{1,0:T(8,128)(2,1)}, u32[]{:S(2)}) copy-start(bf16[512,1024]{1,0:T(8,128)(2,1)} %param.10) | copy-start | bytes 3145732
  7.2 90.7 %all-gather.5.cloned.1.call-start = ((), (), s32[]{:S(2)}) async-start(), calls=%async_computation | async-start | bytes 17301504 | tf_op jit(solution)/shard_map/all_gather | solution.py:65
  14.7 1.3 copy-start.8
  16.0 1.6 copy-start.13
  16.0 193.4 %all-gather.7.cloned.1.call-start = ((), (), s32[]{:S(2)}) async-start(), calls=%async_computation.1 | async-start | bytes 17301504 | tf_op jit(solution)/shard_map/all_gather | solution.py:14
  33.7 0.7 copy-start.11
  97.9 7.8 %copy-start.6 = (bf16[512,1024]{1,0:T(8,128)(2,1)S(1)}, bf16[512,1024]{1,0:T(8,128)(2,1)}, u32[]{:S(2)}) copy-start(bf16[512,1024]{1,0:T(8,128)(2,1)} %param.8) | copy-start | bytes 3145732
  105.8 0.7 copy-start.14
  125.6 4.3 %copy-start.7 = (bf16[512,1024]{1,0:T(8,128)(2,1)S(1)}, bf16[512,1024]{1,0:T(8,128)(2,1)}, u32[]{:S(2)}) copy-start(bf16[512,1024]{1,0:T(8,128)(2,1)} %param.8) | copy-start | bytes 3145732
  129.0 1.0 copy-start.2
  131.2 2.4 copy-start.3
  133.6 1.0 copy-start.12
  134.6 1.4 copy-start.9
  136.0 2.5 copy-start.1
  393.8 2.5 copy-start.10
  394.5 2.0 copy-start.4
  397.9 2.4 copy-start.5
Sparse Core Ops, SparseCore 0:
  16.1 81.7 all-gather.4
  131.4 77.9 all-gather.6
where the time goes:
time: 417 us; the launch traced here: 414 us
  waiting for transfers between devices  123 us (29%)
  loops' own time  105 us (25%)
  local copies, waits for them, and re-layouts  57.2 us (14%)
  other arithmetic  55.7 us (13%)
  matrix products  29.1 us (7%)
  blocking collectives  28.5 us (7%)
  between operations  15 us (4%)
    another operation x1, loops' own time, carried_in(): return lax.fori_loop(0, peers, turn, start)  105 us
    all_gather x1, waiting for transfers between devices, carried_in(): everything = jax.tree.map(lambda part: lax.all_gather(part, axis), shard)  64.4 us
    all_gather x1, waiting for transfers between devices, body(): states = lax.all_gather(piece[None], 'ctx', axis=0, tiled=True)  58.7 us
    select_n x32, other arithmetic, turn(): return jax.tree.map(lambda a, b: jnp.where(reached, a, b), new, before)  41.7 us
    dynamic_slice x64, local copies, waits for them, and re-layouts, turn(): new = combine(before, jax.tree.map(lambda part: part[at], everything))  37.6 us
    unnamed x39, local copies, waits for them, and re-layouts  15.4 us
    unnamed x1, blocking collectives  14.5 us
    psum x1, blocking collectives, body(): lax.psum((jnp.sum(attended * attended, axis=(1, 2)), jnp.sum(scaled * att...  14 us
  transfers between devices with their start and end apart: 2, of which 2 were waited for; matrix products, arithmetic and copies ran while one was open for 5% of the time, Pallas kernels for 0%

commit v1 on v0

v1 whole, which is shorter than its diff:
```python
import functools

import jax
import jax.numpy as jnp
from jax import lax
from jax.experimental import pallas as pl
from jax.experimental.pallas import tpu as pltpu
from jax.sharding import PartitionSpec as P

DH = 128
TILE = 256
epsilon = 1e-05
MESH = pl.DeviceIdType.MESH
F32 = jnp.float32
BF16 = jnp.bfloat16


def nn(a, b):
    return lax.dot_general(a, b, (((1,), (0,)), ((), ())), preferred_element_type=F32)


def nt(a, b):
    return lax.dot_general(a, b, (((1,), (1,)), ((), ())), preferred_element_type=F32)


def tn(a, b):
    return lax.dot_general(a, b, (((0,), (0,)), ((), ())), preferred_element_type=F32)


def equal(a, b):
    return jnp.where(a == b, 1.0, 0.0).astype(F32)


def kernel(
    nctx, nhead,
    q_hbm, k_hbm, v_hbm, dy_hbm, gain_ref, docs_ref,
    normed_hbm, qg_hbm, kg_hbm, vg_hbm,
    q, k, v, dy, qf, kl, vl, oa, att, weights, adj, same, dcol,
    first_col, last_col, inv_col, adj_col, sq_acc, gr_acc,
    piece, sib_piece, total, slices, scanned, landed, to_sib, from_sib, state,
    my_info, sib_info, chip_info, all_info, stat_out, stat_in,
    normed, qg, kgl, vgl, kg, vg,
    in_sem, out_sem, info_send, info_recv, sib_info_sem,
    up_send, up_recv, a_send, a_recv, b_send, b_recv, down_send, down_recv,
    stat_send, stat_recv,
):
    tokens, width = q.shape
    heads = width // DH
    half = heads // 2
    chips = nctx // 2
    rows = half * DH // chips
    per_head = DH // rows
    blocks = tokens // DH
    tiles = tokens // TILE
    me = lax.axis_index("ctx")
    z = lax.axis_index("head")
    chip = lax.div(me, 2)
    core = lax.rem(me, 2)
    sibling = me + 1 - 2 * core
    shift = lax.rem(lax.div(chip, max(per_head, 1)), half)

    def cols(h):
        return pl.ds(pl.multiple_of(h * DH, DH), DH)

    def side(s):
        return pl.ds(pl.multiple_of(s * (width // 2), width // 2), width // 2)

    def slot(i):
        return pl.ds(pl.multiple_of(i * rows, rows), rows)

    def square(h):
        return pl.ds(pl.multiple_of(h * DH, DH), DH)

    def load(i, src, dst, s):
        return pltpu.make_async_copy(src.at[:, side(s)], dst.at[:, side(s)], in_sem.at[i])

    loads = [
        load(0, k_hbm, k, 1 - core), load(1, v_hbm, v, 1 - core),
        load(2, k_hbm, k, core), load(3, v_hbm, v, core),
        load(4, q_hbm, q, 0), load(5, q_hbm, q, 1),
        load(6, dy_hbm, dy, 0), load(7, dy_hbm, dy, 1),
    ]
    for copy in loads:
        copy.start()

    barrier = pltpu.get_barrier_semaphore()
    pl.semaphore_signal(barrier, inc=1, device_id={"ctx": sibling}, device_id_type=MESH)

    def greet_chip(d, carry):
        peer = lax.rem(chip + d, chips)
        pl.semaphore_signal(
            barrier, inc=1, device_id={"ctx": 2 * peer + core}, device_id_type=MESH
        )
        return carry

    def greet_head(d, carry):
        pl.semaphore_signal(
            barrier, inc=1, device_id={"head": lax.rem(z + d, nhead)}, device_id_type=MESH
        )
        return carry

    lax.fori_loop(1, chips, greet_chip, 0)
    lax.fori_loop(1, nhead, greet_head, 0)

    drow = docs_ref[...].astype(F32)
    first_id = drow[:, 0:1]
    last_id = drow[:, tokens - 1 : tokens]
    my_info[0:1, :] = jnp.broadcast_to(first_id, (1, DH))
    my_info[1:2, :] = jnp.broadcast_to(last_id, (1, DH))
    for b in range(blocks):
        block = slice(b * DH, (b + 1) * DH)
        dcol[block, :] = jnp.broadcast_to(drow[:, block], (DH, DH)).T
    first_col[...] = equal(dcol[...], first_id)
    last_col[...] = equal(dcol[...], last_id)

    def make_piece(h):
        last = last_col[...].astype(BF16)
        keys = k[:, cols(h)] * last
        kl[:, cols(h)] = keys
        vl[:, cols(h)] = v[:, cols(h)] * last
        piece[square(h), :] = tn(keys, v[:, cols(h)])

    def push_up(turn, j):
        return pltpu.make_async_remote_copy(
            src_ref=piece.at[square((1 - core) * half + j), :],
            dst_ref=sib_piece.at[turn, square(j), :],
            send_sem=up_send.at[turn, j],
            recv_sem=up_recv.at[turn, j],
            device_id={"ctx": sibling},
            device_id_type=MESH,
        )

    def send_slice(turn, i):
        return pltpu.make_async_remote_copy(
            src_ref=total.at[turn, slot(i), :],
            dst_ref=slices.at[turn, slot(chip), :],
            send_sem=a_send.at[turn, i],
            recv_sem=a_recv.at[turn, chip],
            device_id={"ctx": 2 * i + core},
            device_id_type=MESH,
        )

    def recv_slice(turn, i):
        return pltpu.make_async_remote_copy(
            src_ref=total.at[turn, slot(i), :],
            dst_ref=slices.at[turn, slot(i), :],
            send_sem=a_send.at[turn, i],
            recv_sem=a_recv.at[turn, i],
            device_id={"ctx": 2 * i + core},
            device_id_type=MESH,
        )

    def send_back(turn, i):
        return pltpu.make_async_remote_copy(
            src_ref=scanned.at[turn, slot(i), :],
            dst_ref=landed.at[turn, slot(chip), :],
            send_sem=b_send.at[turn, i],
            recv_sem=b_recv.at[turn, chip],
            device_id={"ctx": 2 * i + core},
            device_id_type=MESH,
        )

    def recv_back(turn, i):
        return pltpu.make_async_remote_copy(
            src_ref=scanned.at[turn, slot(i), :],
            dst_ref=landed.at[turn, slot(i), :],
            send_sem=b_send.at[turn, i],
            recv_sem=b_recv.at[turn, i],
            device_id={"ctx": 2 * i + core},
            device_id_type=MESH,
        )

    def push_down(turn, j):
        return pltpu.make_async_remote_copy(
            src_ref=to_sib.at[turn, square(j), :],
            dst_ref=from_sib.at[turn, square(j), :],
            send_sem=down_send.at[turn, j],
            recv_sem=down_recv.at[turn, j],
            device_id={"ctx": sibling},
            device_id_type=MESH,
        )

    def send_info(d):
        peer = lax.rem(chip + d, chips)
        return pltpu.make_async_remote_copy(
            src_ref=chip_info,
            dst_ref=all_info.at[chip],
            send_sem=info_send.at[peer],
            recv_sem=info_recv.at[chip],
            device_id={"ctx": 2 * peer + core},
            device_id_type=MESH,
        )

    def recv_info(i):
        return pltpu.make_async_remote_copy(
            src_ref=chip_info,
            dst_ref=all_info.at[i],
            send_sem=info_send.at[i],
            recv_sem=info_recv.at[i],
            device_id={"ctx": 2 * i + core},
            device_id_type=MESH,
        )

    def head_order(j):
        return lax.rem(j + shift, half)

    def orders(turn):
        return (0, 1, 2, 3) if turn == 0 else (3, 2, 1, 0)

    def is_near(turn):
        return jnp.full((1, DH), core if turn == 0 else 1 - core, jnp.int32) == 0

    def ascend(turn):
        near_first, near_last, far_first, far_last = orders(turn)
        joined = equal(chip_info[near_last : near_last + 1, :], chip_info[far_last : far_last + 1, :])
        mine = jnp.where(is_near(turn), joined, 1.0)
        theirs = jnp.where(is_near(turn), 1.0, joined)

        def one(j, carry):
            head = head_order(j)
            push_up(turn, head).wait_recv()
            total[turn, square(head), :] = (
                piece[square(core * half + head), :] * mine
                + sib_piece[turn, square(head), :] * theirs
            )
            for s in range(per_head):
                i = head * per_head + s

                @pl.when(i != chip)
                def _():
                    send_slice(turn, i).start()

                @pl.when(i == chip)
                def _():
                    slices[turn, slot(chip), :] = total[turn, slot(chip), :]

            return carry

        lax.fori_loop(0, half, one, 0)

    def scan(turn):
        near_first, _, _, far_last = orders(turn)

        def one(j, carry):
            running, before = carry
            i = j if turn == 0 else chips - 1 - j

            @pl.when(i != chip)
            def _():
                recv_slice(turn, i).wait_recv()

            ids = all_info[i]
            enters = ids[near_first : near_first + 1, :]
            leaves = ids[far_last : far_last + 1, :]
            arriving = running * equal(before, enters)
            scanned[turn, slot(i), :] = arriving

            @pl.when(i != chip)
            def _():
                send_back(turn, i).start()

            @pl.when(i == chip)
            def _():
                landed[turn, slot(chip), :] = arriving

            running = slices[turn, slot(i), :] + running * equal(before, leaves)
            return running, leaves

        lax.fori_loop(
            0, chips, one, (jnp.zeros((rows, DH), F32), jnp.full((1, DH), -1.0, F32))
        )

    def descend(turn):
        near_first, near_last, far_first, far_last = orders(turn)
        next_to = equal(chip_info[near_last : near_last + 1, :], chip_info[far_first : far_first + 1, :])
        through = equal(chip_info[near_first : near_first + 1, :], chip_info[far_first : far_first + 1, :])
        near = is_near(turn)
        own_enter = jnp.where(near, 1.0, through)
        own_sib = jnp.where(near, 0.0, next_to)
        sib_enter = jnp.where(near, through, 1.0)
        sib_own = jnp.where(near, next_to, 0.0)

        def one(j, carry):
            for s in range(per_head):
                i = j * per_head + s

                @pl.when(i != chip)
                def _():
                    recv_back(turn, i).wait_recv()

            entering = landed[turn, square(j), :]
            own = piece[square(core * half + j), :]
            theirs = sib_piece[turn, square(j), :]
            to_sib[turn, square(j), :] = entering * sib_enter + own * sib_own
            push_down(turn, j).start()
            state[turn, square(core * half + j), :] = (
                entering * own_enter + theirs * own_sib
            ).astype(BF16)
            return carry

        lax.fori_loop(0, half, one, 0)

    def land(turn, j):
        push_down(turn, j).wait_recv()
        state[turn, square((1 - core) * half + j), :] = from_sib[turn, square(j), :].astype(BF16)

    def settle(turn):
        def one_head(j, carry):
            push_up(turn, j).wait_send()
            push_down(turn, j).wait_send()
            return carry

        def one_chip(i, carry):
            @pl.when(i != chip)
            def _():
                send_slice(turn, i).wait_send()
                send_back(turn, i).wait_send()

            return carry

        lax.fori_loop(0, half, one_head, 0)
        lax.fori_loop(0, chips, one_chip, 0)

    loads[0].wait()
    loads[1].wait()

    def first_pieces(j, carry):
        make_piece((1 - core) * half + head_order(j))
        return carry

    lax.fori_loop(0, half, first_pieces, 0)
    pl.semaphore_wait(barrier, 1 + (chips - 1) + (nhead - 1))
    sib_ids = pltpu.make_async_remote_copy(
        src_ref=my_info,
        dst_ref=sib_info,
        send_sem=sib_info_sem.at[0],
        recv_sem=sib_info_sem.at[1],
        device_id={"ctx": sibling},
        device_id_type=MESH,
    )
    sib_ids.start()

    def start_up(j, carry):
        push_up(0, head_order(j)).start()
        return carry

    lax.fori_loop(0, half, start_up, 0)
    loads[2].wait()
    loads[3].wait()

    def own_pieces(j, carry):
        make_piece(core * half + head_order(j))
        return carry

    lax.fori_loop(0, half, own_pieces, 0)
    sib_ids.wait()
    near = is_near(0)
    for at in range(2):
        mine, theirs = my_info[at : at + 1, :], sib_info[at : at + 1, :]
        chip_info[at : at + 1, :] = jnp.where(near, mine, theirs)
        chip_info[at + 2 : at + 3, :] = jnp.where(near, theirs, mine)
    all_info[chip] = chip_info[...]

    def start_info(d, carry):
        send_info(d).start()
        return carry

    lax.fori_loop(1, chips, start_info, 0)
    ascend(0)

    for b in range(blocks):
        block = slice(b * DH, (b + 1) * DH)
        later = lax.broadcasted_iota(jnp.int32, (tokens, DH), 0)
        earlier = lax.broadcasted_iota(jnp.int32, (tokens, DH), 1) + b * DH
        ids = jnp.broadcast_to(drow[:, block], (tokens, DH))
        same[:, block] = jnp.where(
            (dcol[...] == ids) & (later >= earlier), 1.0, 0.0
        ).astype(BF16)
    for copy in loads[4:]:
        copy.wait()

    def local_forward(h, carry):
        qf[:, cols(h)] = q[:, cols(h)] * first_col[...].astype(BF16)
        for r in range(tiles):
            here, upto = slice(r * TILE, (r + 1) * TILE), slice(0, (r + 1) * TILE)
            scores = nt(q[here, cols(h)], k[upto, cols(h)])
            masked = scores.astype(BF16) * same[here, upto]
            weights[h, here, upto] = masked
            att[here, cols(h)] = nn(masked, v[upto, cols(h)])
        return carry

    lax.fori_loop(0, half, local_forward, 0)

    def wait_info(d, carry):
        recv_info(lax.rem(chip + d, chips)).wait_recv()
        return carry

    lax.fori_loop(1, chips, wait_info, 0)
    scan(0)
    lax.fori_loop(half, heads, local_forward, 0)
    descend(0)

    sq_acc[...] = jnp.zeros_like(sq_acc)
    gr_acc[...] = jnp.zeros_like(gr_acc)

    def attend(h):
        whole = att[:, cols(h)] + nn(qf[:, cols(h)], state[0, square(h), :])
        att[:, cols(h)] = whole
        scaled = gain_ref[:, cols(h)] * dy[:, cols(h)].astype(F32)
        sq_acc[...] += whole * whole
        gr_acc[...] += scaled * whole

    def attend_own(j, carry):
        attend(core * half + j)
        return carry

    def attend_other(j, carry):
        land(0, j)
        attend((1 - core) * half + j)
        return carry

    lax.fori_loop(0, half, attend_own, 0)
    lax.fori_loop(0, half, attend_other, 0)
    for b in range(blocks):
        block = slice(b * DH, (b + 1) * DH)
        stat_out[b : b + 1, :] = jnp.sum(sq_acc[block, :].T, axis=0, keepdims=True)
        stat_out[blocks + b : blocks + b + 1, :] = jnp.sum(
            gr_acc[block, :].T, axis=0, keepdims=True
        )
    stat_in[z] = stat_out[...]

    def send_stat(d):
        peer = lax.rem(z + d, nhead)
        return pltpu.make_async_remote_copy(
            src_ref=stat_out,
            dst_ref=stat_in.at[z],
            send_sem=stat_send.at[peer],
            recv_sem=stat_recv.at[z],
            device_id={"head": peer},
            device_id_type=MESH,
        )

    def recv_stat(d):
        source = lax.rem(z + nhead - d, nhead)
        return pltpu.make_async_remote_copy(
            src_ref=stat_out,
            dst_ref=stat_in.at[source],
            send_sem=stat_send.at[source],
            recv_sem=stat_recv.at[source],
            device_id={"head": source},
            device_id_type=MESH,
        )

    def start_stat(d, carry):
        send_stat(d).start()
        return carry

    def wait_stat(d, carry):
        recv_stat(d).wait_recv()
        return carry

    lax.fori_loop(1, nhead, start_stat, 0)
    settle(0)
    lax.fori_loop(1, nhead, wait_stat, 0)
    sums = stat_in[0]
    for other in range(1, nhead):
        sums = sums + stat_in[other]
    means = sums / (width * nhead)
    inv = lax.rsqrt(means[0:blocks, :] + epsilon)
    factor = inv * inv * inv * means[blocks : 2 * blocks, :]
    for b in range(blocks):
        block = slice(b * DH, (b + 1) * DH)
        inv_col[block, :] = jnp.broadcast_to(inv[b : b + 1, :], (DH, DH)).T
        adj_col[block, :] = jnp.broadcast_to(factor[b : b + 1, :], (DH, DH)).T

    def adjoint(h):
        scaled = gain_ref[:, cols(h)] * dy[:, cols(h)].astype(F32)
        grads = (inv_col[...] * scaled - att[:, cols(h)] * adj_col[...]).astype(BF16)
        oa[:, cols(h)] = grads
        piece[square(h), :] = tn(grads, qf[:, cols(h)])

    def adjoint_other(j, carry):
        head = head_order(j)
        adjoint((1 - core) * half + head)
        push_up(1, head).start()
        return carry

    def adjoint_own(j, carry):
        adjoint(core * half + head_order(j))
        return carry

    lax.fori_loop(0, half, adjoint_other, 0)
    lax.fori_loop(0, half, adjoint_own, 0)
    ascend(1)

    def local_backward(h, carry):
        grads = oa[:, cols(h)]
        stepped = nt(grads, state[0, square(h), :]) * first_col[...]
        for r in range(tiles):
            here, upto = slice(r * TILE, (r + 1) * TILE), slice(0, (r + 1) * TILE)
            scores = nt(grads[here], v[upto, cols(h)])
            masked = scores.astype(BF16) * same[here, upto]
            adj[here, upto] = masked
            qg[here, cols(h)] = (nn(masked, k[upto, cols(h)]) + stepped[here]).astype(BF16)
        for r in range(tiles):
            here, onward = slice(r * TILE, (r + 1) * TILE), slice(r * TILE, tokens)
            kgl[here, cols(h)] = tn(adj[onward, here], q[onward, cols(h)])
            vgl[here, cols(h)] = tn(weights[h, onward, here], grads[onward])
        normed[:, cols(h)] = (gain_ref[:, cols(h)] * att[:, cols(h)] * inv_col[...]).astype(BF16)
        return carry

    lax.fori_loop(0, half, local_backward, 0)
    scan(1)
    lax.fori_loop(half, heads, local_backward, 0)
    stores = [
        pltpu.make_async_copy(normed, normed_hbm, out_sem.at[0]),
        pltpu.make_async_copy(qg, qg_hbm, out_sem.at[1]),
    ]
    for copy in stores:
        copy.start()
    descend(1)

    def finish(h):
        back = state[1, square(h), :]
        kg[:, cols(h)] = (kgl[:, cols(h)] + nn(vl[:, cols(h)], back)).astype(BF16)
        vg[:, cols(h)] = (vgl[:, cols(h)] + nt(kl[:, cols(h)], back)).astype(BF16)

    def finish_own(j, carry):
        finish(core * half + j)
        return carry

    def finish_other(j, carry):
        land(1, j)
        finish((1 - core) * half + j)
        return carry

    def store(i, src, dst, s):
        return pltpu.make_async_copy(src.at[:, side(s)], dst.at[:, side(s)], out_sem.at[i])

    lax.fori_loop(0, half, finish_own, 0)
    for i, (src, dst) in enumerate(((kg, kg_hbm), (vg, vg_hbm))):
        stores.append(store(2 + i, src, dst, core))
        stores[-1].start()
    lax.fori_loop(0, half, finish_other, 0)
    for i, (src, dst) in enumerate(((kg, kg_hbm), (vg, vg_hbm))):
        stores.append(store(4 + i, src, dst, 1 - core))
        stores[-1].start()

    settle(1)

    def end_info(d, carry):
        send_info(d).wait_send()
        return carry

    def end_stat(d, carry):
        send_stat(d).wait_send()
        return carry

    lax.fori_loop(1, chips, end_info, 0)
    lax.fori_loop(1, nhead, end_stat, 0)
    for copy in stores:
        copy.wait()


def body(nctx, nhead, query_rows, key_rows, value_rows, out_grad, norm_gain, doc_ids):
    tokens, width = query_rows.shape
    heads = width // DH
    half = heads // 2
    chips = nctx // 2
    blocks = tokens // DH
    grid = (tokens, width)
    dma = pltpu.SemaphoreType.DMA
    scratch = [
        *[pltpu.VMEM(grid, BF16)] * 4,
        *[pltpu.VMEM(grid, BF16)] * 4,
        pltpu.VMEM(grid, F32),
        pltpu.VMEM((heads, tokens, tokens), BF16),
        pltpu.VMEM((tokens, tokens), BF16),
        pltpu.VMEM((tokens, tokens), BF16),
        *[pltpu.VMEM((tokens, DH), F32)] * 7,
        pltpu.VMEM((heads * DH, DH), F32),
        *[pltpu.VMEM((2, half * DH, DH), F32)] * 7,
        pltpu.VMEM((2, heads * DH, DH), BF16),
        *[pltpu.VMEM((8, DH), F32)] * 3,
        pltpu.VMEM((chips, 8, DH), F32),
        pltpu.VMEM((2 * blocks, DH), F32),
        pltpu.VMEM((nhead, 2 * blocks, DH), F32),
        *[pltpu.VMEM(grid, BF16)] * 2,
        *[pltpu.VMEM(grid, F32)] * 2,
        *[pltpu.VMEM(grid, BF16)] * 2,
        dma((8,)), dma((6,)), dma((chips,)), dma((chips,)), dma((2,)),
        dma((2, half)), dma((2, half)), dma((2, chips)), dma((2, chips)),
        dma((2, chips)), dma((2, chips)), dma((2, half)), dma((2, half)),
        dma((nhead,)), dma((nhead,)),
    ]
    anywhere = pl.BlockSpec(memory_space=pl.ANY)
    in_vmem = pl.BlockSpec(memory_space=pltpu.VMEM)
    return pl.pallas_call(
        functools.partial(kernel, nctx, nhead),
        out_shape=[jax.ShapeDtypeStruct(grid, BF16)] * 4,
        in_specs=[anywhere] * 4 + [in_vmem] * 2,
        out_specs=[anywhere] * 4,
        scratch_shapes=scratch,
        compiler_params=pltpu.CompilerParams(
            collective_id=0, has_side_effects=True, vmem_limit_bytes=50 * 2**20
        ),
        name="attend",
    )(
        query_rows, key_rows, value_rows, out_grad,
        norm_gain.reshape(1, width), doc_ids.reshape(1, tokens),
    )


def solution(mesh):
    nctx, nhead = mesh.shape["ctx"], mesh.shape["head"]
    placed = (
        P("ctx", "head"),
        P("ctx", "head"),
        P("ctx", "head"),
        P("ctx", "head"),
        P("head"),
        P("ctx"),
    )
    return jax.shard_map(
        functools.partial(body, nctx, nhead),
        mesh=mesh,
        in_specs=placed,
        out_specs=(P("ctx", "head"), P("ctx", "head"), P("ctx", "head"), P("ctx", "head")),
        check_vma=False,
    )
```

time: 417 us -> 56.1 us (0.13)
  waiting for transfers between devices: 123 us -> 0 us
  loops' own time: 105 us -> 0 us
  other arithmetic: 55.7 us -> 0 us
  local copies, waits for them, and re-layouts: 57.2 us -> 5.87 us
  Pallas kernels: 0 us -> 49.4 us
  matrix products: 29.1 us -> 0 us
  blocking collectives: 28.5 us -> 0 us
  between operations: 15 us -> 0.65 us
    all_gather x2 -> x0, waiting for transfers between devices: 123 us -> none  [the longest x1 64.4 us: carried_in(): everything = jax.tree.map(lambda part: lax.all_gather(part, axis), shard)]
    another operation x1 -> x0, loops' own time: 105 us -> none  [carried_in(): return lax.fori_loop(0, peers, turn, start)]
    pallas_call x0 -> x1, Pallas kernels: none -> 49.4 us  [body(): pl.pallas_call(functools.partial(kernel, nctx, nhead), out_shape=[jax.Sha...]
    select_n x32 -> x0, other arithmetic: 41.7 us -> none  [turn(): return jax.tree.map(lambda a, b: jnp.where(reached, a, b), new, before)]
    dynamic_slice x64 -> x0, local copies, waits for them, and re-layouts: 37.6 us -> none  [turn(): new = combine(before, jax.tree.map(lambda part: part[at], everything))]
    dot_general x12 -> x0, matrix products: 29.1 us -> none  [the longest x1 5.15 us: body(): jnp.einsum('hts,shd->thd', weights, values, preferred_element_type=jnp.fl...]
    unnamed x1 -> x0, blocking collectives: 14.5 us -> none
    psum x1 -> x0, blocking collectives: 14 us -> none  [body(): lax.psum((jnp.sum(attended * attended, axis=(1, 2)), jnp.sum(scaled * att...]
  transfers between devices with their start and end apart: 2 -> 0, of which waited for: 2 -> 0; matrix products, arithmetic and copies ran while one was open for 5% -> 0% of each run, Pallas kernels for 0% -> 0%
where the time goes in v1:
time: 56.1 us; the launch traced here: 55.9 us
  Pallas kernels  49.4 us (88%)
  local copies, waits for them, and re-layouts  5.87 us (10%)
  between operations  0.65 us (1%)
    pallas_call x1, Pallas kernels, body(): pl.pallas_call(functools.partial(kernel, nctx, nhead), out_shape=[jax.Sha...  49.4 us
    unnamed x10, local copies, waits for them, and re-layouts  5.87 us

profile of v1, /device:TPU:1, one launch (start us, length us, event | category | flops | bytes accessed | tf_op | source)
XLA Modules:
  0.0 55.9 jit_solution(17902278994110624183)
XLA Ops:
  0.6 0.0 copy-start.1
  0.6 0.7 %copy-done.1 = s32[512]{0:T(512)S(1)} copy-done((s32[512]{0:T(512)S(1)}, s32[512]{0:T(512)}, u32[]{:S(2)}) %copy-start.1) | copy-done | bytes 2072
  1.3 0.0 copy-start
  1.3 0.7 %copy-done = f32[1024]{0:T(1024)S(1)} copy-done((f32[1024]{0:T(1024)S(1)}, f32[1024]{0:T(1024)}, u32[]{:S(2)}) %copy-start) | copy-done | bytes 4120
  2.0 49.4 %attend.1 = (bf16[512,1024]{1,0:T(8,128)(2,1)S(1)}, bf16[512,1024]{1,0:T(8,128)(2,1)S(1)}, bf16[512,1024]{1,0:T(8,128)(2,1)S(1)}, bf16[512,1024]{1,0:T(8,128)(2,1)}) custom-call(bf16[512,1024]{1,0:T(8,128)(2,1)} %q_hbm.1, bf16[512,1024]{1,0:T(8,128)(2,1)} %k_hbm.1, bf16[512,1024]{1,0:T(8,128)(2,1)} %v_hbm.1, bf16[512,1024]{1,0:T(8,128)(2,1)} %dy_hbm.1, ...), custom_call_target="tpu_custom_call" | custom-call | tf_op jit(solution)/shard_map/attend/pallas_call | solution.py:598
  51.4 1.0 %copy.14 = bf16[512,1024]{1,0:T(8,128)(2,1)} copy(bf16[512,1024]{1,0:T(8,128)(2,1)S(1)} %get-tuple-element.8) | data formatting | bytes 2097152
  52.4 1.0 %copy.15 = bf16[512,1024]{1,0:T(8,128)(2,1)} copy(bf16[512,1024]{1,0:T(8,128)(2,1)S(1)} %get-tuple-element.9) | data formatting | bytes 2097152
  53.4 0.0 copy-start.2
  53.4 1.0 %copy.16 = bf16[512,1024]{1,0:T(8,128)(2,1)} copy(bf16[512,1024]{1,0:T(8,128)(2,1)S(1)} %get-tuple-element.10) | data formatting | bytes 2097152
  54.3 0.6 %copy-done.2 = bf16[512,1024]{1,0:T(8,128)(2,1)S(1)} copy-done((bf16[512,1024]{1,0:T(8,128)(2,1)S(1)}, bf16[512,1024]{1,0:T(8,128)(2,1)}, u32[]{:S(2)}) %copy-start.2) | copy-done | bytes 1048600
  55.0 1.0 %copy.17 = bf16[512,1024]{1,0:T(8,128)(2,1)} copy(bf16[512,1024]{1,0:T(8,128)(2,1)S(1)} %copy-done.2) | data formatting | bytes 2097152
Async XLA Ops:
  0.6 0.7 %copy-start.1 = (s32[512]{0:T(512)S(1)}, s32[512]{0:T(512)}, u32[]{:S(2)}) copy-start(s32[512]{0:T(512)} %param.11) | copy-start | bytes 6148
  1.3 0.7 %copy-start = (f32[1024]{0:T(1024)S(1)}, f32[1024]{0:T(1024)}, u32[]{:S(2)}) copy-start(f32[1024]{0:T(1024)} %param.10) | copy-start | bytes 12292
  53.4 1.6 %copy-start.2 = (bf16[512,1024]{1,0:T(8,128)(2,1)S(1)}, bf16[512,1024]{1,0:T(8,128)(2,1)}, u32[]{:S(2)}) copy-start(bf16[512,1024]{1,0:T(8,128)(2,1)} %get-tuple-element.11) | copy-start | bytes 3145732

commit v2 on v0

v2 whole, which is shorter than its diff:
```python
import functools
import math

import jax
import jax.numpy as jnp
from jax import lax
from jax.experimental import pallas as pl
from jax.experimental.pallas import tpu as pltpu
from jax.sharding import PartitionSpec as P

DH = 128
TILE = 256
epsilon = 1e-05
MESH = pl.DeviceIdType.MESH
F32 = jnp.float32
BF16 = jnp.bfloat16


def nn(a, b):
    return lax.dot_general(a, b, (((1,), (0,)), ((), ())), preferred_element_type=F32)


def nt(a, b):
    return lax.dot_general(a, b, (((1,), (1,)), ((), ())), preferred_element_type=F32)


def tn(a, b):
    return lax.dot_general(a, b, (((0,), (0,)), ((), ())), preferred_element_type=F32)


def equal(a, b):
    return jnp.where(a == b, 1.0, 0.0).astype(F32)


def far_first(chips):
    across = math.isqrt(chips)
    along = chips // across

    def hops(offset):
        dy, dx = offset
        return min(dy, along - dy) + min(dx, across - dx)

    offsets = [(dy, dx) for dy in range(along) for dx in range(across) if dy + dx > 0]
    return sorted(offsets, key=hops, reverse=True)


def kernel(
    nctx, nhead,
    q_hbm, k_hbm, v_hbm, dy_hbm, gain_hbm, docs_hbm,
    normed, qg, kgl0, kgl1, vgl0, vgl1, kl, vl, back_state,
    q, k, v, dy, qf, oa, att, weights, adj, same, gain, docs, qf_turned, dcol,
    first_col, last_col, inv_col, adj_col, sq_acc, gr_acc,
    piece, sib_piece, total, slices, scanned, landed, to_sib, from_sib, state,
    my_info, sib_info, chip_info, all_info, stat_out, stat_in,
    in_sem, info_sem, sib_sem, up_send, up_recv, a_send, a_recv, b_send, b_recv,
    down_send, down_recv, stat_sem,
):
    tokens, width = q.shape
    heads = width // DH
    half = heads // 2
    chips = nctx // 2
    across = math.isqrt(chips)
    along = chips // across
    rows = half * DH // chips
    blocks = tokens // DH
    tiles = tokens // TILE
    me = lax.axis_index("ctx")
    z = lax.axis_index("head")
    chip = lax.div(me, 2)
    core = lax.rem(me, 2)
    sibling = me + 1 - 2 * core
    mine, other = core * half, (1 - core) * half
    everyone = (chips - 1) * rows

    def cols(h):
        return pl.ds(pl.multiple_of(h * DH, DH), DH)

    def side(s):
        return pl.ds(pl.multiple_of(s * (width // 2), width // 2), width // 2)

    def slot(i):
        return pl.ds(pl.multiple_of(i * rows, rows), rows)

    def half_of(h):
        return pl.ds(pl.multiple_of(h * DH, half * DH), half * DH)

    def chip_at(offset):
        y = lax.rem(lax.div(chip, across) + offset[0], along)
        x = lax.rem(lax.rem(chip, across) + offset[1], across)
        return y * across + x

    def to_chip(i):
        return {"ctx": 2 * i + core}

    chip_offsets = far_first(chips)
    head_offsets = sorted(range(1, nhead), key=lambda d: -min(d, nhead - d))

    def load(i, src, dst, s):
        return pltpu.make_async_copy(src.at[:, side(s)], dst.at[:, side(s)], in_sem.at[i])

    first_loads = [load(0, k_hbm, k, 1 - core), load(1, v_hbm, v, 1 - core)]
    docs_load = pltpu.make_async_copy(docs_hbm, docs, in_sem.at[2])
    own_loads = [load(3, k_hbm, k, core), load(4, v_hbm, v, core)]
    later_loads = [
        pltpu.make_async_copy(q_hbm, q, in_sem.at[5]),
        pltpu.make_async_copy(dy_hbm, dy, in_sem.at[6]),
        pltpu.make_async_copy(gain_hbm, gain, in_sem.at[7]),
    ]
    docs_load.start()
    for copy in first_loads:
        copy.start()

    barrier = pltpu.get_barrier_semaphore()

    def greet(device):
        pl.semaphore_signal(barrier, inc=1, device_id=device, device_id_type=MESH)

    for offset in chip_offsets:
        greet(to_chip(chip_at(offset)))
    for offset in head_offsets:
        greet({"head": lax.rem(z + offset, nhead)})
    greet({"ctx": sibling})
    for copy in own_loads + later_loads:
        copy.start()

    docs_load.wait()
    drow = docs[...].astype(F32)
    first_id = drow[:, 0:1]
    last_id = drow[:, tokens - 1 : tokens]
    my_info[0:1, :] = jnp.broadcast_to(first_id, (1, DH))
    my_info[1:2, :] = jnp.broadcast_to(last_id, (1, DH))
    for b in range(blocks):
        block = slice(b * DH, (b + 1) * DH)
        dcol[block, :] = jnp.broadcast_to(drow[:, block], (DH, DH)).T
    first_col[...] = equal(dcol[...], first_id)
    last_col[...] = equal(dcol[...], last_id).astype(BF16)

    def to_sibling(src, dst, send_sem, recv_sem):
        return pltpu.make_async_remote_copy(
            src_ref=src,
            dst_ref=dst,
            send_sem=send_sem,
            recv_sem=recv_sem,
            device_id={"ctx": sibling},
            device_id_type=MESH,
        )

    def push_up(turn):
        return to_sibling(
            piece.at[turn, half_of(other), :], sib_piece.at[turn],
            up_send.at[turn], up_recv.at[turn],
        )

    def push_down(turn):
        return to_sibling(
            to_sib.at[turn], from_sib.at[turn], down_send.at[turn], down_recv.at[turn]
        )

    def spread(src, dst, send_sem, recv_sem):
        for offset in chip_offsets:
            i = chip_at(offset)
            pltpu.make_async_remote_copy(
                src_ref=src.at[slot(i), :],
                dst_ref=dst.at[slot(chip), :],
                send_sem=send_sem,
                recv_sem=recv_sem,
                device_id=to_chip(i),
                device_id_type=MESH,
            ).start()

    def spread_whole(src, dst, send_sem, recv_sem):
        return pltpu.make_async_remote_copy(
            src_ref=src.at[0:everyone, :],
            dst_ref=dst.at[0:everyone, :],
            send_sem=send_sem,
            recv_sem=recv_sem,
            device_id={"ctx": sibling},
            device_id_type=MESH,
        )

    def slices_whole(turn):
        return spread_whole(total.at[turn], slices.at[turn], a_send.at[turn], a_recv.at[turn])

    def back_whole(turn):
        return spread_whole(scanned.at[turn], landed.at[turn], b_send.at[turn], b_recv.at[turn])

    def info_whole():
        return pltpu.make_async_remote_copy(
            src_ref=all_info.at[0 : chips - 1],
            dst_ref=all_info.at[0 : chips - 1],
            send_sem=info_sem.at[0],
            recv_sem=info_sem.at[1],
            device_id={"ctx": sibling},
            device_id_type=MESH,
        )

    def orders(turn):
        return (0, 1, 2, 3) if turn == 0 else (3, 2, 1, 0)

    def is_near(turn):
        return jnp.full((1, DH), core if turn == 0 else 1 - core, jnp.int32) == 0

    def ids_of(row):
        return chip_info[row : row + 1, :]

    def ascend(turn):
        _, near_last, _, far_last = orders(turn)
        joined = equal(ids_of(near_last), ids_of(far_last))
        own_share = jnp.where(is_near(turn), joined, 1.0)
        sib_share = jnp.where(is_near(turn), 1.0, joined)
        push_up(turn).wait_recv()
        total[turn] = piece[turn, half_of(mine), :] * own_share + sib_piece[turn] * sib_share
        spread(total.at[turn], slices.at[turn], a_send.at[turn], a_recv.at[turn])
        slices[turn, slot(chip), :] = total[turn, slot(chip), :]

    def scan(turn):
        near_first, _, _, far_last = orders(turn)
        slices_whole(turn).wait_recv()
        running = jnp.zeros((rows, DH), F32)
        before = jnp.full((1, DH), -1.0, F32)
        for j in range(chips):
            i = j if turn == 0 else chips - 1 - j
            ids = all_info[i]
            enters = ids[near_first : near_first + 1, :]
            leaves = ids[far_last : far_last + 1, :]
            here = slice(i * rows, (i + 1) * rows)
            scanned[turn, here, :] = running * equal(before, enters)
            running = slices[turn, here, :] + running * equal(before, leaves)
            before = leaves
        spread(scanned.at[turn], landed.at[turn], b_send.at[turn], b_recv.at[turn])
        landed[turn, slot(chip), :] = scanned[turn, slot(chip), :]

    def descend(turn, into):
        near_first, near_last, far_first, _ = orders(turn)
        next_to = equal(ids_of(near_last), ids_of(far_first))
        through = equal(ids_of(near_first), ids_of(far_first))
        near = is_near(turn)
        own_enter = jnp.where(near, 1.0, through)
        own_sib = jnp.where(near, 0.0, next_to)
        sib_enter = jnp.where(near, through, 1.0)
        sib_own = jnp.where(near, next_to, 0.0)
        back_whole(turn).wait_recv()
        to_sib[turn] = landed[turn] * sib_enter + piece[turn, half_of(mine), :] * sib_own
        push_down(turn).start()
        into[half_of(mine), :] = (landed[turn] * own_enter + sib_piece[turn] * own_sib).astype(BF16)

    def land(turn, into):
        push_down(turn).wait_recv()
        into[half_of(other), :] = from_sib[turn].astype(BF16)

    def settle(turn):
        push_up(turn).wait_send()
        push_down(turn).wait_send()
        slices_whole(turn).wait_send()
        back_whole(turn).wait_send()

    def make_piece(h):
        piece[0, cols(h), :] = tn(k[:, cols(h)] * last_col[...], v[:, cols(h)])

    for copy in first_loads:
        copy.wait()
    for j in range(half):
        make_piece(other + j)
    pl.semaphore_wait(barrier, 1 + (chips - 1) + (nhead - 1))
    sib_ids = to_sibling(my_info, sib_info, sib_sem.at[0], sib_sem.at[1])
    sib_ids.start()
    push_up(0).start()
    for copy in own_loads:
        copy.wait()
    for j in range(half):
        make_piece(mine + j)
    sib_ids.wait_recv()
    near = is_near(0)
    for at in range(2):
        here, there = my_info[at : at + 1, :], sib_info[at : at + 1, :]
        chip_info[at : at + 1, :] = jnp.where(near, here, there)
        chip_info[at + 2 : at + 3, :] = jnp.where(near, there, here)
    for offset in chip_offsets:
        pltpu.make_async_remote_copy(
            src_ref=chip_info,
            dst_ref=all_info.at[chip],
            send_sem=info_sem.at[0],
            recv_sem=info_sem.at[1],
            device_id=to_chip(chip_at(offset)),
            device_id_type=MESH,
        ).start()
    all_info[chip] = chip_info[...]
    ascend(0)

    later = lax.broadcasted_iota(jnp.int32, (tokens, DH), 0)
    for b in range(blocks):
        block = slice(b * DH, (b + 1) * DH)
        earlier = lax.broadcasted_iota(jnp.int32, (tokens, DH), 1) + b * DH
        ids = jnp.broadcast_to(drow[:, block], (tokens, DH))
        same[:, block] = jnp.where((dcol[...] == ids) & (later >= earlier), 1.0, 0.0).astype(BF16)
    for copy in later_loads:
        copy.wait()

    def local_forward(h, carry):
        kl[:, cols(h)] = k[:, cols(h)] * last_col[...]
        vl[:, cols(h)] = v[:, cols(h)] * last_col[...]
        firsts = q[:, cols(h)] * first_col[...].astype(BF16)
        qf[:, cols(h)] = firsts
        qf_turned[cols(h), :] = firsts.T
        for r in range(tiles):
            here, upto = slice(r * TILE, (r + 1) * TILE), slice(0, (r + 1) * TILE)
            scores = nt(q[here, cols(h)], k[upto, cols(h)])
            masked = scores.astype(BF16) * same[here, upto]
            weights[h, here, upto] = masked
            att[here, cols(h)] = nn(masked, v[upto, cols(h)])
        return carry

    lax.fori_loop(0, heads, local_forward, 0, unroll=2)
    info_whole().wait_recv()
    scan(0)
    descend(0, state)

    def attend(h, first):
        whole = att[:, cols(h)] + nn(qf[:, cols(h)], state[cols(h), :])
        att[:, cols(h)] = whole
        scaled = gain[:, cols(h)] * dy[:, cols(h)].astype(F32)
        squares, grads = whole * whole, scaled * whole
        sq_acc[...] = squares if first else sq_acc[...] + squares
        gr_acc[...] = grads if first else gr_acc[...] + grads

    for j in range(half):
        attend(mine + j, j == 0)
    land(0, state)
    for j in range(half):
        attend(other + j, False)
    for b in range(blocks):
        block = slice(b * DH, (b + 1) * DH)
        stat_out[b : b + 1, :] = jnp.sum(sq_acc[block, :].T, axis=0, keepdims=True)
        stat_out[blocks + b : blocks + b + 1, :] = jnp.sum(
            gr_acc[block, :].T, axis=0, keepdims=True
        )
    for offset in head_offsets:
        pltpu.make_async_remote_copy(
            src_ref=stat_out,
            dst_ref=stat_in.at[z],
            send_sem=stat_sem.at[0],
            recv_sem=stat_sem.at[1],
            device_id={"head": lax.rem(z + offset, nhead)},
            device_id_type=MESH,
        ).start()
    stat_in[z] = stat_out[...]
    settle(0)
    stat_whole = pltpu.make_async_remote_copy(
        src_ref=stat_in.at[0 : nhead - 1],
        dst_ref=stat_in.at[0 : nhead - 1],
        send_sem=stat_sem.at[0],
        recv_sem=stat_sem.at[1],
        device_id={"ctx": sibling},
        device_id_type=MESH,
    )
    stat_whole.wait_recv()
    sums = stat_in[0]
    for at in range(1, nhead):
        sums = sums + stat_in[at]
    means = sums / (width * nhead)
    inv = lax.rsqrt(means[0:blocks, :] + epsilon)
    factor = inv * inv * inv * means[blocks : 2 * blocks, :]
    for b in range(blocks):
        block = slice(b * DH, (b + 1) * DH)
        inv_col[block, :] = jnp.broadcast_to(inv[b : b + 1, :], (DH, DH)).T
        adj_col[block, :] = jnp.broadcast_to(factor[b : b + 1, :], (DH, DH)).T

    def adjoint(h):
        scaled = gain[:, cols(h)] * dy[:, cols(h)].astype(F32)
        grads = (inv_col[...] * scaled - att[:, cols(h)] * adj_col[...]).astype(BF16)
        oa[:, cols(h)] = grads
        piece[1, cols(h), :] = nn(qf_turned[cols(h), :], grads)

    for j in range(half):
        adjoint(other + j)
    push_up(1).start()
    for j in range(half):
        adjoint(mine + j)
    ascend(1)

    def local_backward(j, carry, base, kgl, vgl):
        h = base + j
        grads = oa[:, cols(h)]
        stepped = nt(grads, state[cols(h), :]) * first_col[...]
        for r in range(tiles):
            here, upto = slice(r * TILE, (r + 1) * TILE), slice(0, (r + 1) * TILE)
            scores = nt(grads[here], v[upto, cols(h)])
            masked = scores.astype(BF16) * same[here, upto]
            adj[here, upto] = masked
            qg[here, cols(h)] = (nn(masked, k[upto, cols(h)]) + stepped[here]).astype(BF16)
        for r in range(tiles):
            here, onward = slice(r * TILE, (r + 1) * TILE), slice(r * TILE, tokens)
            kgl[here, cols(j)] = tn(adj[onward, here], q[onward, cols(h)])
            vgl[here, cols(j)] = tn(weights[h, onward, here], grads[onward])
        normed[:, cols(h)] = (gain[:, cols(h)] * att[:, cols(h)] * inv_col[...]).astype(BF16)
        return carry

    lower = functools.partial(local_backward, base=0, kgl=kgl0, vgl=vgl0)
    upper = functools.partial(local_backward, base=half, kgl=kgl1, vgl=vgl1)
    lax.fori_loop(0, half, lower, 0, unroll=2)
    scan(1)
    lax.fori_loop(0, half, upper, 0, unroll=2)
    descend(1, back_state)
    sib_ids.wait_send()
    info_whole().wait_send()
    stat_whole.wait_send()
    land(1, back_state)
    settle(1)


def finish(
    normed, qg, kgl0, kgl1, vgl0, vgl1, kl, vl, back_state,
    normed_hbm, qg_hbm, kg_hbm, vg_hbm,
    kg, vg, out_sem,
):
    heads = kg.shape[1] // DH
    stores = [
        pltpu.make_async_copy(normed, normed_hbm, out_sem.at[0]),
        pltpu.make_async_copy(qg, qg_hbm, out_sem.at[1]),
    ]
    for copy in stores:
        copy.start()
    parts = 2
    per_part = heads // parts
    for part, (kgl, vgl) in enumerate(((kgl0, vgl0), (kgl1, vgl1))):
        for j in range(per_part):
            here = slice(j * DH, (j + 1) * DH)
            at = slice((part * per_part + j) * DH, (part * per_part + j + 1) * DH)
            back = back_state[at, :]
            kg[:, at] = (kgl[:, here] + nt(vl[:, at], back)).astype(BF16)
            vg[:, at] = (vgl[:, here] + nn(kl[:, at], back)).astype(BF16)
        done = slice(part * per_part * DH, (part + 1) * per_part * DH)
        for i, (src, dst) in enumerate(((kg, kg_hbm), (vg, vg_hbm))):
            copy = pltpu.make_async_copy(
                src.at[:, done], dst.at[:, done], out_sem.at[2 + 2 * part + i]
            )
            copy.start()
            stores.append(copy)
    for copy in stores:
        copy.wait()


def body(nctx, nhead, query_rows, key_rows, value_rows, out_grad, norm_gain, doc_ids):
    tokens, width = query_rows.shape
    heads = width // DH
    half = heads // 2
    chips = nctx // 2
    blocks = tokens // DH
    grid = (tokens, width)
    dma = pltpu.SemaphoreType.DMA
    scratch = [
        *[pltpu.VMEM(grid, BF16)] * 6,
        pltpu.VMEM(grid, F32),
        pltpu.VMEM((heads, tokens, tokens), BF16),
        pltpu.VMEM((tokens, tokens), BF16),
        pltpu.VMEM((tokens, tokens), BF16),
        pltpu.VMEM((1, width), F32),
        pltpu.VMEM((1, tokens), jnp.int32),
        pltpu.VMEM((heads * DH, tokens), BF16),
        *[pltpu.VMEM((tokens, DH), F32)] * 2,
        pltpu.VMEM((tokens, DH), BF16),
        *[pltpu.VMEM((tokens, DH), F32)] * 4,
        pltpu.VMEM((2, heads * DH, DH), F32),
        *[pltpu.VMEM((2, half * DH, DH), F32)] * 7,
        pltpu.VMEM((heads * DH, DH), BF16),
        *[pltpu.VMEM((8, DH), F32)] * 3,
        pltpu.VMEM((chips, 8, DH), F32),
        pltpu.VMEM((2 * blocks, DH), F32),
        pltpu.VMEM((nhead, 2 * blocks, DH), F32),
        dma((8,)),
        *[dma((2,))] * 11,
    ]
    arrays = (
        query_rows, key_rows, value_rows, out_grad,
        norm_gain.reshape(1, width), doc_ids.reshape(1, tokens),
    )
    anywhere = pl.BlockSpec(memory_space=pl.ANY)
    in_hbm = pl.BlockSpec(memory_space=pltpu.HBM)
    in_vmem = pl.BlockSpec(memory_space=pltpu.VMEM)
    parts = pl.pallas_call(
        functools.partial(kernel, nctx, nhead),
        out_shape=[
            *[jax.ShapeDtypeStruct(grid, BF16)] * 2,
            *[jax.ShapeDtypeStruct((tokens, width // 2), F32)] * 4,
            *[jax.ShapeDtypeStruct(grid, BF16)] * 2,
            jax.ShapeDtypeStruct((heads * DH, DH), BF16),
        ],
        in_specs=[in_hbm] * 6,
        out_specs=[in_vmem] * 9,
        scratch_shapes=scratch,
        compiler_params=pltpu.CompilerParams(
            collective_id=0, has_side_effects=True, vmem_limit_bytes=44 * 2**20
        ),
        name="attend",
    )(*[pltpu.with_memory_space_constraint(array, pltpu.HBM) for array in arrays])
    return pl.pallas_call(
        finish,
        out_shape=[jax.ShapeDtypeStruct(grid, BF16)] * 4,
        in_specs=[in_vmem] * 9,
        out_specs=[anywhere] * 4,
        scratch_shapes=[*[pltpu.VMEM(grid, BF16)] * 2, dma((6,))],
        compiler_params=pltpu.CompilerParams(vmem_limit_bytes=16 * 2**20),
        name="finish",
    )(*parts)


def solution(mesh):
    nctx, nhead = mesh.shape["ctx"], mesh.shape["head"]
    placed = (
        P("ctx", "head"),
        P("ctx", "head"),
        P("ctx", "head"),
        P("ctx", "head"),
        P("head"),
        P("ctx"),
    )
    return jax.shard_map(
        functools.partial(body, nctx, nhead),
        mesh=mesh,
        in_specs=placed,
        out_specs=(P("ctx", "head"), P("ctx", "head"), P("ctx", "head"), P("ctx", "head")),
        check_vma=False,
    )
```

time: 417 us -> 49.1 us (0.12)
  waiting for transfers between devices: 123 us -> 0 us
  loops' own time: 105 us -> 0 us
  local copies, waits for them, and re-layouts: 57.2 us -> 0 us
  other arithmetic: 55.7 us -> 0 us
  Pallas kernels: 0 us -> 48.4 us
  matrix products: 29.1 us -> 0 us
  blocking collectives: 28.5 us -> 0 us
  between operations: 15 us -> 0.64 us
    all_gather x2 -> x0, waiting for transfers between devices: 123 us -> none  [the longest x1 64.4 us: carried_in(): everything = jax.tree.map(lambda part: lax.all_gather(part, axis), shard)]
    another operation x1 -> x0, loops' own time: 105 us -> none  [carried_in(): return lax.fori_loop(0, peers, turn, start)]
    pallas_call x0 -> x2, Pallas kernels: none -> 48.4 us  [the longest x1 46.4 us: body(): pl.pallas_call(functools.partial(kernel, nctx, nhead), out_shape=[*[jax.S...]
    select_n x32 -> x0, other arithmetic: 41.7 us -> none  [turn(): return jax.tree.map(lambda a, b: jnp.where(reached, a, b), new, before)]
    dynamic_slice x64 -> x0, local copies, waits for them, and re-layouts: 37.6 us -> none  [turn(): new = combine(before, jax.tree.map(lambda part: part[at], everything))]
    dot_general x12 -> x0, matrix products: 29.1 us -> none  [the longest x1 5.15 us: body(): jnp.einsum('hts,shd->thd', weights, values, preferred_element_type=jnp.fl...]
    unnamed x39 -> x0, local copies, waits for them, and re-layouts: 15.4 us -> none
    unnamed x1 -> x0, blocking collectives: 14.5 us -> none
  transfers between devices with their start and end apart: 2 -> 0, of which waited for: 2 -> 0; matrix products, arithmetic and copies ran while one was open for 5% -> 0% of each run, Pallas kernels for 0% -> 0%
where the time goes in v2:
time: 49.1 us; the launch traced here: 49 us
  Pallas kernels  48.4 us (99%)
  between operations  0.64 us (1%)
    pallas_call x1, Pallas kernels, body(): pl.pallas_call(functools.partial(kernel, nctx, nhead), out_shape=[*[jax.S...  46.4 us
    pallas_call x1, Pallas kernels, body(): pl.pallas_call(finish, out_shape=[jax.ShapeDtypeStruct(grid, BF16)] * 4,...  2.06 us

profile of v2, /device:TPU:1, one launch (start us, length us, event | category | flops | bytes accessed | tf_op | source)
XLA Modules:
  0.0 49.0 jit_solution(8741751966529810770)
XLA Ops:
  0.6 46.4 %attend.1 = (bf16[512,1024]{1,0:T(8,128)(2,1)S(1)}, bf16[512,1024]{1,0:T(8,128)(2,1)S(1)}, f32[512,512]{1,0:T(8,128)S(1)}, f32[512,512]{1,0:T(8,128)S(1)}, f32[5...) custom-call(bf16[512,1024]{1,0:T(8,128)(2,1)} %q_hbm.1, ...), custom_call_target="tpu_custom_call" | custom-call | tf_op jit(solution)/shard_map/attend/pallas_call | solution.py:480
  47.0 2.1 %finish.1 = (bf16[512,1024]{1,0:T(8,128)(2,1)}, bf16[512,1024]{1,0:T(8,128)(2,1)}, bf16[512,1024]{1,0:T(8,128)(2,1)}, bf16[512,1024]{1,0:T(8,128)(2,1)}) custom-call(bf16[512,1024]{1,0:T(8,128)(2,1)S(1)} %get-tuple-element.13.normed, bf16[512,1024]{1,0:T(8,128)(2,1)S(1)} %get-tuple-element.14.qg, f32[512,512]{1,0:T(8,128)S(1)} %get-tuple-element.15.kgl0, ...), custom_call_target="tpu_custom_call" | custom-call | tf_op jit(solution)/shard_map/finish/pallas_call | solution.py:496

commit v3 on v2

v3 whole, which is shorter than its diff:
```python
import functools
import math

import jax
import jax.numpy as jnp
from jax import lax
from jax.experimental import pallas as pl
from jax.experimental.pallas import tpu as pltpu
from jax.sharding import PartitionSpec as P

DH = 128
TILE = 256
epsilon = 1e-05
MESH = pl.DeviceIdType.MESH
F32 = jnp.float32
BF16 = jnp.bfloat16


def nn(a, b):
    return lax.dot_general(a, b, (((1,), (0,)), ((), ())), preferred_element_type=F32)


def nt(a, b):
    return lax.dot_general(a, b, (((1,), (1,)), ((), ())), preferred_element_type=F32)


def tn(a, b):
    return lax.dot_general(a, b, (((0,), (0,)), ((), ())), preferred_element_type=F32)


def equal(a, b):
    return jnp.where(a == b, 1.0, 0.0).astype(F32)


def row_sums(values):
    ones = jnp.ones((8, DH), BF16)
    high = values.astype(BF16)
    low = (values - high.astype(F32)).astype(BF16)
    return (nt(ones, high) + nt(ones, low))[0:1, :]


def far_first(chips):
    across = math.isqrt(chips)
    along = chips // across

    def hops(offset):
        dy, dx = offset
        return min(dy, along - dy) + min(dx, across - dx)

    offsets = [(dy, dx) for dy in range(along) for dx in range(across) if dy + dx > 0]
    return sorted(offsets, key=hops, reverse=True)


def kernel(
    nctx, nhead,
    q_hbm, k_hbm, v_hbm, dy_hbm, gain_hbm, docs_hbm,
    normed, qg, kg_own, vg_own, kgl_other, vgl_other, kl_other, vl_other, back_other,
    q, k, v, dy, qf, oa, att, scaled, weights, adj, same, gain, docs, qf_turned, dcol,
    first_col, last_col, inv_col, adj_col, sq_acc, gr_acc,
    piece, sib_piece, total, slices, scanned, landed, to_sib, from_sib, state,
    kgl_own, vgl_own, kl_own, vl_own, back_own, my_info, sib_info, chip_info, stat_out, stat_in,
    in_sem, sib_sem, up_send, up_recv, a_send, a_recv, b_send, b_recv,
    down_send, down_recv, stat_sem,
):
    tokens, width = q.shape
    heads = width // DH
    half = heads // 2
    chips = nctx // 2
    across = math.isqrt(chips)
    along = chips // across
    rows = half * DH // chips
    blocks = tokens // DH
    tiles = tokens // TILE
    me = lax.axis_index("ctx")
    z = lax.axis_index("head")
    chip = lax.div(me, 2)
    core = lax.rem(me, 2)
    sibling = me + 1 - 2 * core
    mine, other = core * half, (1 - core) * half
    here_y, here_x = lax.div(chip, across), lax.rem(chip, across)
    row_offsets = sorted(range(along), key=lambda d: -min(d, along - d))
    column_offsets = sorted(range(across), key=lambda d: -min(d, across - d))
    groups = [row_offsets[: along // 2], row_offsets[along // 2 :]]

    def cols(h):
        return pl.ds(pl.multiple_of(h * DH, DH), DH)

    def side(s):
        return pl.ds(pl.multiple_of(s * (width // 2), width // 2), width // 2)

    def slot(i):
        return pl.ds(pl.multiple_of(i * rows, rows), rows)

    def chip_at(offset):
        y = lax.rem(here_y + offset[0], along)
        x = lax.rem(here_x + offset[1], across)
        return y * across + x

    def head_at(d):
        return lax.rem(here_y + d, along)

    def to_chip(i):
        return {"ctx": 2 * i + core}

    chip_offsets = far_first(chips)
    head_offsets = sorted(range(1, nhead), key=lambda d: -min(d, nhead - d))

    def load(i, src, dst, s):
        return pltpu.make_async_copy(src.at[:, side(s)], dst.at[:, side(s)], in_sem.at[i])

    first_loads = [load(0, k_hbm, k, 1 - core), load(1, v_hbm, v, 1 - core)]
    docs_load = pltpu.make_async_copy(docs_hbm, docs, in_sem.at[2])
    own_loads = [load(3, k_hbm, k, core), load(4, v_hbm, v, core)]
    later_loads = [
        pltpu.make_async_copy(q_hbm, q, in_sem.at[5]),
        pltpu.make_async_copy(dy_hbm, dy, in_sem.at[6]),
        pltpu.make_async_copy(gain_hbm, gain, in_sem.at[7]),
    ]
    docs_load.start()
    for copy in first_loads:
        copy.start()

    barrier = pltpu.get_barrier_semaphore()

    def greet(device):
        pl.semaphore_signal(barrier, inc=1, device_id=device, device_id_type=MESH)

    for offset in chip_offsets:
        greet({"ctx": 2 * chip_at(offset)})
    for offset in head_offsets:
        greet({"ctx": 2 * chip, "head": lax.rem(z + offset, nhead)})
    greet({"ctx": sibling})
    for copy in own_loads + later_loads:
        copy.start()

    docs_load.wait()
    drow = docs[...].astype(F32)
    first_id = drow[:, 0:1]
    last_id = drow[:, tokens - 1 : tokens]
    my_info[0:1, :] = jnp.broadcast_to(first_id, (1, DH))
    my_info[1:2, :] = jnp.broadcast_to(last_id, (1, DH))
    for b in range(blocks):
        block = slice(b * DH, (b + 1) * DH)
        dcol[block, :] = jnp.broadcast_to(drow[:, block], (DH, DH)).T
    first_col[...] = equal(dcol[...], first_id)
    last_col[...] = equal(dcol[...], last_id).astype(BF16)

    def to_sibling(src, dst, send_sem, recv_sem):
        return pltpu.make_async_remote_copy(
            src_ref=src,
            dst_ref=dst,
            send_sem=send_sem,
            recv_sem=recv_sem,
            device_id={"ctx": sibling},
            device_id_type=MESH,
        )

    def push_up(g, d):
        at = cols(other + head_at(d))
        return to_sibling(
            piece.at[1, at, :], sib_piece.at[1, at, :], up_send.at[1], up_recv.at[1, g]
        )

    def up_heads(turn, g, first, last):
        at = slice(first * DH, last * DH)
        return to_sibling(
            piece.at[turn, at, :], sib_piece.at[turn, at, :],
            up_send.at[turn], up_recv.at[turn, g],
        )

    def push_down(turn, head):
        return to_sibling(
            to_sib.at[turn, cols(head), :], from_sib.at[turn, cols(head), :],
            down_send.at[turn], down_recv.at[turn, head],
        )

    def send_slice(src, dst, send_sem, recv_sem, device):
        pltpu.make_async_remote_copy(
            src_ref=src,
            dst_ref=dst,
            send_sem=send_sem,
            recv_sem=recv_sem,
            device_id=device,
            device_id_type=MESH,
        ).start()

    def sent_rows(turn):
        return slice(0, rows + 8) if turn == 0 else slice(0, rows)

    def slices_whole(turn, count):
        part = (slice(0, count), sent_rows(turn))
        return to_sibling(total.at[part], total.at[part], a_send.at[turn], a_recv.at[turn])

    def back_whole(turn, count, row):
        part = (turn, slice(0, count * rows))
        return to_sibling(
            scanned.at[part], landed.at[part], b_send.at[turn], b_recv.at[turn, row]
        )

    def orders(turn):
        return (0, 1, 2, 3) if turn == 0 else (3, 2, 1, 0)

    def is_near(turn):
        return jnp.full((1, DH), core if turn == 0 else 1 - core, jnp.int32) == 0

    def ids_of(row):
        return chip_info[row : row + 1, :]

    def add_up(turn, head, place):
        _, near_last, _, far_last = orders(turn)
        joined = equal(ids_of(near_last), ids_of(far_last))
        own_share = jnp.where(is_near(turn), joined, 1.0)
        sib_share = jnp.where(is_near(turn), 1.0, joined)
        for x in range(across):
            part = pl.ds(pl.multiple_of(head * DH + x * rows, rows), rows)
            total[place + x, 0:rows, :] = (
                piece[turn, part, :] * own_share + sib_piece[turn, part, :] * sib_share
            )

    def ascend_forward():
        @pl.when(core == 1)
        def _():
            pl.semaphore_wait(barrier, 1)
            sib_ids.start()
            up_heads(0, 0, 0, heads).start()

        @pl.when(core == 0)
        def _():
            sib_ids.wait_recv()
            chip_info[0:2, :] = my_info[0:2, :]
            chip_info[2:4, :] = sib_info[0:2, :]
            up_heads(0, 0, 0, heads).wait_recv()
            for head in range(heads):
                add_up(0, head, head * across)
            for i in range(2 * chips):
                total[i, rows : rows + 8, :] = chip_info[...]
            pl.semaphore_wait(barrier, 1 + 2 * (chips - 1) + 2 * (nhead - 1))
            for offset in chip_offsets:
                i = chip_at(offset)
                for a in range(2):
                    send_slice(
                        total.at[a * chips + i], slices.at[0, chip],
                        a_send.at[0], a_recv.at[0], {"ctx": 2 * i + a},
                    )
            send_slice(
                total.at[chips + chip], slices.at[0, chip],
                a_send.at[0], a_recv.at[0], {"ctx": sibling},
            )
            up_heads(0, 0, half, heads).start()
            slices[0, chip] = total[chip]

    def ascend_backward():
        for g, group in enumerate(groups):
            up_heads(1, g, 0, len(group)).wait_recv()
            for d in group:
                head = head_at(d)
                add_up(1, mine + head, 2 * chips + head * across)
            for offset in chip_offsets:
                if offset[0] in group:
                    i = chip_at(offset)
                    send_slice(
                        total.at[2 * chips + i, sent_rows(1)], slices.at[1, chip, sent_rows(1)],
                        a_send.at[1], a_recv.at[1], to_chip(i),
                    )
        slices[1, chip] = total[2 * chips + chip]

    def scan(turn):
        near_first, _, _, far_last = orders(turn)
        if turn == 0:

            @pl.when(core == 0)
            def _():
                slices_whole(0, chips - 1).wait_recv()

            @pl.when(core == 1)
            def _():
                slices_whole(0, chips).wait_recv()
                up_heads(0, 0, half, heads).wait_recv()
                chip_info[...] = slices[0, chip, rows : rows + 8, :]

        else:
            slices_whole(1, chips - 1).wait_recv()
        running = jnp.zeros((rows, DH), F32)
        before = jnp.full((1, DH), -1.0, F32)
        for j in range(chips):
            i = j if turn == 0 else chips - 1 - j
            ids = slices[0, i, rows : rows + 8, :]
            enters = ids[near_first : near_first + 1, :]
            leaves = ids[far_last : far_last + 1, :]
            here = slice(i * rows, (i + 1) * rows)
            scanned[turn, here, :] = running * equal(before, enters)
            running = slices[turn, i, 0:rows, :] + running * equal(before, leaves)
            before = leaves
        for offset in chip_offsets:
            i = chip_at(offset)
            send_slice(
                scanned.at[turn, slot(i), :], landed.at[turn, slot(chip), :],
                b_send.at[turn], b_recv.at[turn, here_y], to_chip(i),
            )
        landed[turn, slot(chip), :] = scanned[turn, slot(chip), :]

    def descend(turn, into, then):
        near_first, near_last, far_first, _ = orders(turn)
        next_to = equal(ids_of(near_last), ids_of(far_first))
        through = equal(ids_of(near_first), ids_of(far_first))
        near = is_near(turn)
        own_enter = jnp.where(near, 1.0, through)
        own_sib = jnp.where(near, 0.0, next_to)
        sib_enter = jnp.where(near, through, 1.0)
        sib_own = jnp.where(near, next_to, 0.0)
        for d in reversed(row_offsets):
            head = head_at(d)
            at = cols(head)
            back_whole(turn, across - (d == 0), head).wait_recv()
            to_sib[turn, at, :] = (
                landed[turn, at, :] * sib_enter + piece[turn, cols(mine + head), :] * sib_own
            )
            push_down(turn, head).start()
            beyond = sib_piece[turn, cols(mine + head), :]
            into(head, landed[turn, at, :] * own_enter + beyond * own_sib)
            then(head)

    sib_ids = to_sibling(my_info, sib_info, sib_sem.at[0], sib_sem.at[1])

    def settle(turn):
        whole = to_sibling(
            to_sib.at[turn], from_sib.at[turn], down_send.at[turn], down_recv.at[turn, 0]
        )
        whole.wait_send()
        back_whole(turn, chips - 1, 0).wait_send()
        if turn == 0:

            @pl.when(core == 0)
            def _():
                up_heads(0, 0, half, heads).wait_send()
                slices_whole(0, 2 * chips - 1).wait_send()

            @pl.when(core == 1)
            def _():
                up_heads(0, 0, 0, heads).wait_send()
                sib_ids.wait_send()

        else:
            up_heads(1, 0, 0, half).wait_send()
            slices_whole(1, chips - 1).wait_send()

    def make_piece(h):
        piece[0, cols(h), :] = tn(k[:, cols(h)] * last_col[...], v[:, cols(h)])

    for copy in first_loads:
        copy.wait()
    for j in range(half):
        make_piece(other + j)
    for copy in own_loads:
        copy.wait()
    for j in range(half):
        make_piece(mine + j)
    ascend_forward()

    later = lax.broadcasted_iota(jnp.int32, (tokens, DH), 0)
    for b in range(blocks):
        block = slice(b * DH, (b + 1) * DH)
        earlier = lax.broadcasted_iota(jnp.int32, (tokens, DH), 1) + b * DH
        ids = jnp.broadcast_to(drow[:, block], (tokens, DH))
        same[:, block] = jnp.where((dcol[...] == ids) & (later >= earlier), 1.0, 0.0).astype(BF16)
    for copy in later_loads:
        copy.wait()

    def local_forward(h, carry):
        firsts = q[:, cols(h)] * first_col[...].astype(BF16)
        qf[:, cols(h)] = firsts
        qf_turned[cols(h), :] = firsts.T
        scaled[:, cols(h)] = gain[:, cols(h)] * dy[:, cols(h)].astype(F32)
        for r in range(tiles):
            here, upto = slice(r * TILE, (r + 1) * TILE), slice(0, (r + 1) * TILE)
            scores = nt(q[here, cols(h)], k[upto, cols(h)])
            masked = scores.astype(BF16) * same[here, upto]
            weights[h, here, upto] = masked
            att[here, cols(h)] = nn(masked, v[upto, cols(h)])
        return carry

    lax.fori_loop(0, heads, local_forward, 0, unroll=2)
    scan(0)

    def attend(h):
        whole = att[:, cols(h)] + nn(qf[:, cols(h)], state[cols(h), :])
        att[:, cols(h)] = whole
        squares, grads = whole * whole, scaled[:, cols(h)] * whole
        sq_acc[...] += squares
        gr_acc[...] += grads

    def enter(head, block):
        state[cols(mine + head), :] = block.astype(BF16)

    sq_acc[...] = jnp.zeros_like(sq_acc)
    gr_acc[...] = jnp.zeros_like(gr_acc)
    descend(0, enter, lambda head: attend(mine + head))
    arrivals = [head_at(d) for d in reversed(row_offsets)]
    for group in (arrivals[:-1], arrivals[-1:]):
        for head in group:
            push_down(0, head).wait_recv()
        for head in group:
            state[cols(other + head), :] = from_sib[0, cols(head), :].astype(BF16)
            attend(other + head)
    square_sums, grad_sums = row_sums(sq_acc[...]), row_sums(gr_acc[...])
    for b in range(blocks):
        block = slice(b * DH, (b + 1) * DH)
        stat_out[b : b + 1, :] = square_sums[:, block]
        stat_out[blocks + b : blocks + b + 1, :] = grad_sums[:, block]
    for offset in head_offsets:
        pltpu.make_async_remote_copy(
            src_ref=stat_out,
            dst_ref=stat_in.at[z],
            send_sem=stat_sem.at[0],
            recv_sem=stat_sem.at[1],
            device_id={"head": lax.rem(z + offset, nhead)},
            device_id_type=MESH,
        ).start()
    stat_in[z] = stat_out[...]
    settle(0)
    stat_whole = pltpu.make_async_remote_copy(
        src_ref=stat_in.at[0 : nhead - 1],
        dst_ref=stat_in.at[0 : nhead - 1],
        send_sem=stat_sem.at[0],
        recv_sem=stat_sem.at[1],
        device_id={"ctx": sibling},
        device_id_type=MESH,
    )
    stat_whole.wait_recv()
    sums = stat_in[0]
    for at in range(1, nhead):
        sums = sums + stat_in[at]
    means = sums / (width * nhead)
    inv = lax.rsqrt(means[0:blocks, :] + epsilon)
    factor = inv * inv * inv * means[blocks : 2 * blocks, :]
    turned = jnp.concatenate([inv, factor] * (DH // (2 * blocks)), axis=0).T
    for b in range(blocks):
        block = slice(b * DH, (b + 1) * DH)
        inv_col[block, :] = jnp.broadcast_to(turned[:, b : b + 1], (DH, DH))
        adj_col[block, :] = jnp.broadcast_to(turned[:, blocks + b : blocks + b + 1], (DH, DH))

    def adjoint(h):
        grads = (inv_col[...] * scaled[:, cols(h)] - att[:, cols(h)] * adj_col[...]).astype(BF16)
        oa[:, cols(h)] = grads
        piece[1, cols(h), :] = nn(qf_turned[cols(h), :], grads)

    for g, group in enumerate(groups):
        for d in group:
            adjoint(other + head_at(d))
        for d in group:
            push_up(g, d).start()
    for j in range(half):
        adjoint(mine + j)
    ascend_backward()

    def local_backward(j, carry, base, kgl, vgl, kl, vl):
        h = base + j
        kl[:, cols(j)] = k[:, cols(h)] * last_col[...]
        vl[:, cols(j)] = v[:, cols(h)] * last_col[...]
        grads = oa[:, cols(h)]
        stepped = nt(grads, state[cols(h), :]) * first_col[...]
        for r in range(tiles):
            here, upto = slice(r * TILE, (r + 1) * TILE), slice(0, (r + 1) * TILE)
            scores = nt(grads[here], v[upto, cols(h)])
            masked = scores.astype(BF16) * same[here, upto]
            adj[here, upto] = masked
            qg[here, cols(h)] = (nn(masked, k[upto, cols(h)]) + stepped[here]).astype(BF16)
        for r in range(tiles):
            here, onward = slice(r * TILE, (r + 1) * TILE), slice(r * TILE, tokens)
            kgl[here, cols(j)] = tn(adj[onward, here], q[onward, cols(h)])
            vgl[here, cols(j)] = tn(weights[h, onward, here], grads[onward])
        normed[:, cols(h)] = (gain[:, cols(h)] * att[:, cols(h)] * inv_col[...]).astype(BF16)
        return carry

    own_half = functools.partial(
        local_backward, base=mine, kgl=kgl_own, vgl=vgl_own, kl=kl_own, vl=vl_own
    )
    other_half = functools.partial(
        local_backward, base=other, kgl=kgl_other, vgl=vgl_other, kl=kl_other, vl=vl_other
    )
    lax.fori_loop(0, half, own_half, 0, unroll=2)
    scan(1)
    lax.fori_loop(0, half, other_half, 0, unroll=2)

    def enter_back(head, block):
        back_own[cols(head), :] = block.astype(BF16)

    descend(1, enter_back, lambda head: None)
    last_products(kg_own, vg_own, kgl_own, vgl_own, kl_own, vl_own, back_own)
    stat_whole.wait_send()
    for head in arrivals:
        push_down(1, head).wait_recv()
    back_other[...] = from_sib[1].astype(BF16)
    settle(1)


def last_products(kg, vg, kgl, vgl, kl, vl, back_state):
    for h in range(kg.shape[1] // DH):
        at = slice(h * DH, (h + 1) * DH)
        back = back_state[at, :]
        kg[:, at] = (kgl[:, at] + nt(vl[:, at], back)).astype(BF16)
        vg[:, at] = (vgl[:, at] + nn(kl[:, at], back)).astype(BF16)


def finish(
    normed, qg, kg_own, vg_own, kgl_other, vgl_other, kl_other, vl_other, back_other,
    normed_hbm, qg_hbm, kg_hbm, vg_hbm,
    kg_other, vg_other, out_sem,
):
    core = lax.rem(lax.axis_index("ctx"), 2)
    part = kg_other.shape[1]

    def side(s):
        return pl.ds(pl.multiple_of(s * part, part), part)

    stores = [
        pltpu.make_async_copy(normed, normed_hbm, out_sem.at[0]),
        pltpu.make_async_copy(qg, qg_hbm, out_sem.at[1]),
        pltpu.make_async_copy(kg_own, kg_hbm.at[:, side(core)], out_sem.at[2]),
        pltpu.make_async_copy(vg_own, vg_hbm.at[:, side(core)], out_sem.at[3]),
    ]
    for copy in stores:
        copy.start()
    last_products(kg_other, vg_other, kgl_other, vgl_other, kl_other, vl_other, back_other)
    for i, (src, dst) in enumerate(((kg_other, kg_hbm), (vg_other, vg_hbm))):
        copy = pltpu.make_async_copy(src, dst.at[:, side(1 - core)], out_sem.at[4 + i])
        copy.start()
        stores.append(copy)
    for copy in stores:
        copy.wait()


def body(nctx, nhead, query_rows, key_rows, value_rows, out_grad, norm_gain, doc_ids):
    tokens, width = query_rows.shape
    heads = width // DH
    half = heads // 2
    chips = nctx // 2
    rows = half * DH // chips
    blocks = tokens // DH
    grid = (tokens, width)
    half_grid = (tokens, width // 2)
    dma = pltpu.SemaphoreType.DMA
    scratch = [
        *[pltpu.VMEM(grid, BF16)] * 6,
        *[pltpu.VMEM(grid, F32)] * 2,
        pltpu.VMEM((heads, tokens, tokens), BF16),
        pltpu.VMEM((tokens, tokens), BF16),
        pltpu.VMEM((tokens, tokens), BF16),
        pltpu.VMEM((1, width), F32),
        pltpu.VMEM((1, tokens), jnp.int32),
        pltpu.VMEM((heads * DH, tokens), BF16),
        *[pltpu.VMEM((tokens, DH), F32)] * 2,
        pltpu.VMEM((tokens, DH), BF16),
        *[pltpu.VMEM((tokens, DH), F32)] * 4,
        pltpu.VMEM((2, heads * DH, DH), F32),
        pltpu.VMEM((2, heads * DH, DH), F32),
        pltpu.VMEM((3 * chips, rows + 8, DH), F32),
        pltpu.VMEM((2, chips, rows + 8, DH), F32),
        *[pltpu.VMEM((2, half * DH, DH), F32)] * 4,
        pltpu.VMEM((heads * DH, DH), BF16),
        *[pltpu.VMEM(half_grid, F32)] * 2,
        *[pltpu.VMEM(half_grid, BF16)] * 2,
        pltpu.VMEM((half * DH, DH), BF16),
        *[pltpu.VMEM((8, DH), F32)] * 3,
        pltpu.VMEM((2 * blocks, DH), F32),
        pltpu.VMEM((nhead, 2 * blocks, DH), F32),
        dma((8,)),
        *[dma((2,))] * 2,
        dma((2, 2)),
        *[dma((2,))] * 3,
        dma((2, half)),
        dma((2,)),
        dma((2, half)),
        dma((2,)),
    ]
    arrays = (
        query_rows, key_rows, value_rows, out_grad,
        norm_gain.reshape(1, width), doc_ids.reshape(1, tokens),
    )
    anywhere = pl.BlockSpec(memory_space=pl.ANY)
    in_hbm = pl.BlockSpec(memory_space=pltpu.HBM)
    in_vmem = pl.BlockSpec(memory_space=pltpu.VMEM)
    parts = pl.pallas_call(
        functools.partial(kernel, nctx, nhead),
        out_shape=[
            *[jax.ShapeDtypeStruct(grid, BF16)] * 2,
            *[jax.ShapeDtypeStruct(half_grid, BF16)] * 2,
            *[jax.ShapeDtypeStruct(half_grid, F32)] * 2,
            *[jax.ShapeDtypeStruct(half_grid, BF16)] * 2,
            jax.ShapeDtypeStruct((half * DH, DH), BF16),
        ],
        in_specs=[in_hbm] * 6,
        out_specs=[in_vmem] * 9,
        scratch_shapes=scratch,
        compiler_params=pltpu.CompilerParams(
            collective_id=0, has_side_effects=True, vmem_limit_bytes=44 * 2**20
        ),
        name="attend",
    )(*[pltpu.with_memory_space_constraint(array, pltpu.HBM) for array in arrays])
    return pl.pallas_call(
        finish,
        out_shape=[jax.ShapeDtypeStruct(grid, BF16)] * 4,
        in_specs=[in_vmem] * 9,
        out_specs=[anywhere] * 4,
        scratch_shapes=[*[pltpu.VMEM(half_grid, BF16)] * 2, dma((6,))],
        compiler_params=pltpu.CompilerParams(vmem_limit_bytes=16 * 2**20),
        name="finish",
    )(*parts)


def solution(mesh):
    nctx, nhead = mesh.shape["ctx"], mesh.shape["head"]
    placed = (
        P("ctx", "head"),
        P("ctx", "head"),
        P("ctx", "head"),
        P("ctx", "head"),
        P("head"),
        P("ctx"),
    )
    return jax.shard_map(
        functools.partial(body, nctx, nhead),
        mesh=mesh,
        in_specs=placed,
        out_specs=(P("ctx", "head"), P("ctx", "head"), P("ctx", "head"), P("ctx", "head")),
        check_vma=False,
    )
```

time: 49.1 us -> 48.8 us (level)
    pallas_call x1, Pallas kernels: 46.4 us -> 45.7 us  [body(): pl.pallas_call(functools.partial(kernel, nctx, nhead), out_shape=[*[jax.S...]
where the time goes in v3:
time: 48.8 us; the launch traced here: 48.7 us
  Pallas kernels  48.1 us (99%)
  between operations  0.64 us (1%)
    pallas_call x1, Pallas kernels, body(): pl.pallas_call(functools.partial(kernel, nctx, nhead), out_shape=[*[jax.S...  45.7 us
    pallas_call x1, Pallas kernels, body(): pl.pallas_call(finish, out_shape=[jax.ShapeDtypeStruct(grid, BF16)] * 4,...  2.32 us

profile of v3, /device:TPU:1, one launch (start us, length us, event | category | flops | bytes accessed | tf_op | source)
XLA Modules:
  0.0 48.7 jit_solution(14764953971028334062)
XLA Ops:
  0.6 45.7 %attend.1 = (bf16[512,1024]{1,0:T(8,128)(2,1)S(1)}, bf16[512,1024]{1,0:T(8,128)(2,1)S(1)}, bf16[512,512]{1,0:T(8,128)(2,1)S(1)}, bf16[512,512]{1,0:T(8,128)(2,1)...) custom-call(bf16[512,1024]{1,0:T(8,128)(2,1)} %q_hbm.1, ...), custom_call_target="tpu_custom_call" | custom-call | tf_op jit(solution)/shard_map/attend/pallas_call | solution.py:583
  46.4 2.3 %finish.1 = (bf16[512,1024]{1,0:T(8,128)(2,1)}, bf16[512,1024]{1,0:T(8,128)(2,1)}, bf16[512,1024]{1,0:T(8,128)(2,1)}, bf16[512,1024]{1,0:T(8,128)(2,1)}) custom-call(bf16[512,1024]{1,0:T(8,128)(2,1)S(1)} %get-tuple-element.13.normed, bf16[512,1024]{1,0:T(8,128)(2,1)S(1)} %get-tuple-element.14.qg, bf16[512,512]{1,0:T(8,128)(2,1)S(1)} %get-tuple-element.15.kg_own, ...), custom_call_target="tpu_custom_call" | custom-call | tf_op jit(solution)/shard_map/finish/pallas_call | solution.py:600

commit v4 on v3

--- a/solution.py
+++ b/solution.py
@@ -54,13 +54,15 @@
 def kernel(
     nctx, nhead,
     q_hbm, k_hbm, v_hbm, dy_hbm, gain_hbm, docs_hbm,
-    normed, qg, kg_own, vg_own, kgl_other, vgl_other, kl_other, vl_other, back_other,
+    normed, qg, kgl0, kgl1, vgl0, vgl1, kl, vl, back_state,
     q, k, v, dy, qf, oa, att, scaled, weights, adj, same, gain, docs, qf_turned, dcol,
     first_col, last_col, inv_col, adj_col, sq_acc, gr_acc,
     piece, sib_piece, total, slices, scanned, landed, to_sib, from_sib, state,
-    kgl_own, vgl_own, kl_own, vl_own, back_own, my_info, sib_info, chip_info, stat_out, stat_in,
+    my_info, sib_info, chip_info, stat_out, stat_in, stat_sum,
+    qf_wide, qf_in, att_sib, scaled_sib, qf_sib, turned_sib, state_sib,
+    sq_sib, gr_sib, inv_sib, adj_sib,
     in_sem, sib_sem, up_send, up_recv, a_send, a_recv, b_send, b_recv,
-    down_send, down_recv, stat_sem,
+    down_send, down_recv, stat_sem, swap_send, swap_recv,
 ):
     tokens, width = q.shape
     heads = width // DH
@@ -80,7 +82,6 @@
     here_y, here_x = lax.div(chip, across), lax.rem(chip, across)
     row_offsets = sorted(range(along), key=lambda d: -min(d, along - d))
     column_offsets = sorted(range(across), key=lambda d: -min(d, across - d))
-    groups = [row_offsets[: along // 2], row_offsets[along // 2 :]]
 
     def cols(h):
         return pl.ds(pl.multiple_of(h * DH, DH), DH)
@@ -117,7 +118,7 @@
         pltpu.make_async_copy(gain_hbm, gain, in_sem.at[7]),
     ]
     docs_load.start()
-    for copy in first_loads:
+    for copy in first_loads + own_loads:
         copy.start()
 
     barrier = pltpu.get_barrier_semaphore()
@@ -130,7 +131,7 @@
     for offset in head_offsets:
         greet({"ctx": 2 * chip, "head": lax.rem(z + offset, nhead)})
     greet({"ctx": sibling})
-    for copy in own_loads + later_loads:
+    for copy in later_loads:
         copy.start()
 
     docs_load.wait()
@@ -155,12 +156,6 @@
             device_id_type=MESH,
         )
 
-    def push_up(g, d):
-        at = cols(other + head_at(d))
-        return to_sibling(
-            piece.at[1, at, :], sib_piece.at[1, at, :], up_send.at[1], up_recv.at[1, g]
-        )
-
     def up_heads(turn, g, first, last):
         at = slice(first * DH, last * DH)
         return to_sibling(
@@ -196,6 +191,14 @@
         return to_sibling(
             scanned.at[part], landed.at[part], b_send.at[turn], b_recv.at[turn, row]
         )
+
+    def swap(n):
+        src, dst = (
+            (scaled.at[:, side(1 - core)], scaled_sib),
+            (qf_wide, qf_in),
+            (att.at[:, side(1 - core)], att_sib),
+        )[n]
+        return to_sibling(src, dst, swap_send.at[n], swap_recv.at[n])
 
     def orders(turn):
         return (0, 1, 2, 3) if turn == 0 else (3, 2, 1, 0)
@@ -218,19 +221,36 @@
             )
 
     def ascend_forward():
+        for copy in first_loads:
+            copy.wait()
+
         @pl.when(core == 1)
         def _():
+            for h in range(half):
+                make_piece(h)
             pl.semaphore_wait(barrier, 1)
             sib_ids.start()
-            up_heads(0, 0, 0, heads).start()
+            up_heads(0, 0, 0, half).start()
+            for copy in own_loads:
+                copy.wait()
+            for h in range(half, heads):
+                make_piece(h)
+            up_heads(0, 1, half, heads).start()
 
         @pl.when(core == 0)
         def _():
+            for copy in own_loads:
+                copy.wait()
+            for h in range(heads):
+                make_piece(h)
             sib_ids.wait_recv()
             chip_info[0:2, :] = my_info[0:2, :]
             chip_info[2:4, :] = sib_info[0:2, :]
-            up_heads(0, 0, 0, heads).wait_recv()
-            for head in range(heads):
+            up_heads(0, 0, 0, half).wait_recv()
+            for head in range(half):
+                add_up(0, head, head * across)
+            up_heads(0, 1, half, heads).wait_recv()
+            for head in range(half, heads):
                 add_up(0, head, head * across)
             for i in range(2 * chips):
                 total[i, rows : rows + 8, :] = chip_info[...]
@@ -250,18 +270,14 @@
             slices[0, chip] = total[chip]
 
     def ascend_backward():
-        for g, group in enumerate(groups):
-            up_heads(1, g, 0, len(group)).wait_recv()
-            for d in group:
-                head = head_at(d)
-                add_up(1, mine + head, 2 * chips + head * across)
-            for offset in chip_offsets:
-                if offset[0] in group:
-                    i = chip_at(offset)
-                    send_slice(
-                        total.at[2 * chips + i, sent_rows(1)], slices.at[1, chip, sent_rows(1)],
-                        a_send.at[1], a_recv.at[1], to_chip(i),
-                    )
+        for head in range(half):
+            add_up(1, mine + head, 2 * chips + head * across)
+        for offset in chip_offsets:
+            i = chip_at(offset)
+            send_slice(
+                total.at[2 * chips + i, sent_rows(1)], slices.at[1, chip, sent_rows(1)],
+                a_send.at[1], a_recv.at[1], to_chip(i),
+            )
         slices[1, chip] = total[2 * chips + chip]
 
     def scan(turn):
@@ -299,7 +315,7 @@
             )
         landed[turn, slot(chip), :] = scanned[turn, slot(chip), :]
 
-    def descend(turn, into, then):
+    def descend(turn, into):
         near_first, near_last, far_first, _ = orders(turn)
         next_to = equal(ids_of(near_last), ids_of(far_first))
         through = equal(ids_of(near_first), ids_of(far_first))
@@ -318,7 +334,6 @@
             push_down(turn, head).start()
             beyond = sib_piece[turn, cols(mine + head), :]
             into(head, landed[turn, at, :] * own_enter + beyond * own_sib)
-            then(head)
 
     sib_ids = to_sibling(my_info, sib_info, sib_sem.at[0], sib_sem.at[1])
 
@@ -340,21 +355,14 @@
                 up_heads(0, 0, 0, heads).wait_send()
                 sib_ids.wait_send()
 
+            for n in range(3):
+                swap(n).wait_send()
         else:
-            up_heads(1, 0, 0, half).wait_send()
             slices_whole(1, chips - 1).wait_send()
 
     def make_piece(h):
         piece[0, cols(h), :] = tn(k[:, cols(h)] * last_col[...], v[:, cols(h)])
 
-    for copy in first_loads:
-        copy.wait()
-    for j in range(half):
-        make_piece(other + j)
-    for copy in own_loads:
-        copy.wait()
-    for j in range(half):
-        make_piece(mine + j)
     ascend_forward()
 
     later = lax.broadcasted_iota(jnp.int32, (tokens, DH), 0)
@@ -366,11 +374,23 @@
     for copy in later_loads:
         copy.wait()
 
-    def local_forward(h, carry):
-        firsts = q[:, cols(h)] * first_col[...].astype(BF16)
-        qf[:, cols(h)] = firsts
-        qf_turned[cols(h), :] = firsts.T
+    def prepare(j, carry, base):
+        h = base + j
+        qf[:, cols(h)] = q[:, cols(h)] * first_col[...].astype(BF16)
         scaled[:, cols(h)] = gain[:, cols(h)] * dy[:, cols(h)].astype(F32)
+        return carry
+
+    def widen(j, carry):
+        qf_wide[:, cols(j)] = qf[:, cols(other + j)].astype(F32)
+        return carry
+
+    lax.fori_loop(0, half, functools.partial(prepare, base=other), 0)
+    lax.fori_loop(0, half, widen, 0)
+    swap(0).start()
+    swap(1).start()
+
+    def local_forward(j, carry, base):
+        h = base + j
         for r in range(tiles):
             here, upto = slice(r * TILE, (r + 1) * TILE), slice(0, (r + 1) * TILE)
             scores = nt(q[here, cols(h)], k[upto, cols(h)])
@@ -379,84 +399,112 @@
             att[here, cols(h)] = nn(masked, v[upto, cols(h)])
         return carry
 
-    lax.fori_loop(0, heads, local_forward, 0, unroll=2)
+    lax.fori_loop(0, half, functools.partial(local_forward, base=other), 0, unroll=2)
+    swap(2).start()
     scan(0)
-
-    def attend(h):
-        whole = att[:, cols(h)] + nn(qf[:, cols(h)], state[cols(h), :])
-        att[:, cols(h)] = whole
-        squares, grads = whole * whole, scaled[:, cols(h)] * whole
-        sq_acc[...] += squares
-        gr_acc[...] += grads
+    lax.fori_loop(0, half, functools.partial(prepare, base=mine), 0)
+    lax.fori_loop(0, half, functools.partial(local_forward, base=mine), 0, unroll=2)
+    for n in range(3):
+        swap(n).wait_recv()
+
+    def turn_queries(j, carry):
+        queries = qf_in[:, cols(j)].astype(BF16)
+        qf_sib[:, cols(j)] = queries
+        turned_sib[cols(j), :] = queries.T
+        qf_turned[cols(j), :] = qf[:, cols(mine + j)].T
+        return carry
+
+    lax.fori_loop(0, half, turn_queries, 0)
 
     def enter(head, block):
         state[cols(mine + head), :] = block.astype(BF16)
 
+    descend(0, enter)
     sq_acc[...] = jnp.zeros_like(sq_acc)
     gr_acc[...] = jnp.zeros_like(gr_acc)
-    descend(0, enter, lambda head: attend(mine + head))
-    arrivals = [head_at(d) for d in reversed(row_offsets)]
-    for group in (arrivals[:-1], arrivals[-1:]):
-        for head in group:
-            push_down(0, head).wait_recv()
-        for head in group:
-            state[cols(other + head), :] = from_sib[0, cols(head), :].astype(BF16)
-            attend(other + head)
-    square_sums, grad_sums = row_sums(sq_acc[...]), row_sums(gr_acc[...])
-    for b in range(blocks):
-        block = slice(b * DH, (b + 1) * DH)
-        stat_out[b : b + 1, :] = square_sums[:, block]
-        stat_out[blocks + b : blocks + b + 1, :] = grad_sums[:, block]
-    for offset in head_offsets:
+    sq_sib[...] = jnp.zeros_like(sq_sib)
+    gr_sib[...] = jnp.zeros_like(gr_sib)
+    state_sib[...] = to_sib[0].astype(BF16)
+    for j in range(half):
+        whole = att[:, cols(mine + j)] + nn(qf[:, cols(mine + j)], state[cols(mine + j), :])
+        att[:, cols(mine + j)] = whole
+        sq_acc[...] += whole * whole
+        gr_acc[...] += scaled[:, cols(mine + j)] * whole
+    for j in range(half):
+        whole = att_sib[:, cols(j)] + nn(qf_sib[:, cols(j)], state_sib[cols(j), :])
+        att_sib[:, cols(j)] = whole
+        sq_sib[...] += whole * whole
+        gr_sib[...] += scaled_sib[:, cols(j)] * whole
+    for at, squares, grads in ((core, sq_acc, gr_acc), (1 - core, sq_sib, gr_sib)):
+        square_sums, grad_sums = row_sums(squares[...]), row_sums(grads[...])
+        for b in range(blocks):
+            block = slice(b * DH, (b + 1) * DH)
+            stat_out[at, b : b + 1, :] = square_sums[:, block]
+            stat_out[at, blocks + b : blocks + b + 1, :] = grad_sums[:, block]
+
+    def send_stat(device):
         pltpu.make_async_remote_copy(
             src_ref=stat_out,
-            dst_ref=stat_in.at[z],
+            dst_ref=stat_in.at[2 * z + core],
             send_sem=stat_sem.at[0],
             recv_sem=stat_sem.at[1],
-            device_id={"head": lax.rem(z + offset, nhead)},
+            device_id=device,
             device_id_type=MESH,
         ).start()
-    stat_in[z] = stat_out[...]
+
+    for offset in head_offsets:
+        for a in (core, 1 - core):
+            send_stat({"ctx": 2 * chip + a, "head": lax.rem(z + offset, nhead)})
+    send_stat({"ctx": sibling})
+    stat_in[2 * z + core] = stat_out[...]
     settle(0)
-    stat_whole = pltpu.make_async_remote_copy(
-        src_ref=stat_in.at[0 : nhead - 1],
-        dst_ref=stat_in.at[0 : nhead - 1],
-        send_sem=stat_sem.at[0],
-        recv_sem=stat_sem.at[1],
-        device_id={"ctx": sibling},
-        device_id_type=MESH,
+    for d in reversed(row_offsets):
+        head = head_at(d)
+        push_down(0, head).wait_recv()
+        state[cols(other + head), :] = from_sib[0, cols(head), :].astype(BF16)
+    for j in range(half):
+        att[:, cols(other + j)] += nn(qf[:, cols(other + j)], state[cols(other + j), :])
+    stat_whole = to_sibling(
+        stat_in.at[0 : 2 * nhead - 1], stat_in.at[0 : 2 * nhead - 1],
+        stat_sem.at[0], stat_sem.at[1],
     )
     stat_whole.wait_recv()
     sums = stat_in[0]
-    for at in range(1, nhead):
+    for at in range(1, 2 * nhead):
         sums = sums + stat_in[at]
-    means = sums / (width * nhead)
-    inv = lax.rsqrt(means[0:blocks, :] + epsilon)
-    factor = inv * inv * inv * means[blocks : 2 * blocks, :]
-    turned = jnp.concatenate([inv, factor] * (DH // (2 * blocks)), axis=0).T
-    for b in range(blocks):
-        block = slice(b * DH, (b + 1) * DH)
-        inv_col[block, :] = jnp.broadcast_to(turned[:, b : b + 1], (DH, DH))
-        adj_col[block, :] = jnp.broadcast_to(turned[:, blocks + b : blocks + b + 1], (DH, DH))
+    stat_sum[...] = sums / (width * nhead)
+    for at, inv_to, adj_to in ((core, inv_col, adj_col), (1 - core, inv_sib, adj_sib)):
+        means = stat_sum[at]
+        inv = lax.rsqrt(means[0:blocks, :] + epsilon)
+        factor = inv * inv * inv * means[blocks : 2 * blocks, :]
+        turned = jnp.concatenate([inv, factor] * (DH // (2 * blocks)), axis=0).T
+        for b in range(blocks):
+            block = slice(b * DH, (b + 1) * DH)
+            inv_to[block, :] = jnp.broadcast_to(turned[:, b : b + 1], (DH, DH))
+            adj_to[block, :] = jnp.broadcast_to(
+                turned[:, blocks + b : blocks + b + 1], (DH, DH)
+            )
 
     def adjoint(h):
-        grads = (inv_col[...] * scaled[:, cols(h)] - att[:, cols(h)] * adj_col[...]).astype(BF16)
-        oa[:, cols(h)] = grads
-        piece[1, cols(h), :] = nn(qf_turned[cols(h), :], grads)
-
-    for g, group in enumerate(groups):
-        for d in group:
-            adjoint(other + head_at(d))
-        for d in group:
-            push_up(g, d).start()
+        return (inv_col[...] * scaled[:, cols(h)] - att[:, cols(h)] * adj_col[...]).astype(BF16)
+
     for j in range(half):
-        adjoint(mine + j)
+        grads = adjoint(mine + j)
+        oa[:, cols(mine + j)] = grads
+        piece[1, cols(mine + j), :] = nn(qf_turned[cols(j), :], grads)
+    for j in range(half):
+        grads = (
+            inv_sib[...] * scaled_sib[:, cols(j)] - att_sib[:, cols(j)] * adj_sib[...]
+        ).astype(BF16)
+        sib_piece[1, cols(mine + j), :] = nn(turned_sib[cols(j), :], grads)
     ascend_backward()
-
-    def local_backward(j, carry, base, kgl, vgl, kl, vl):
+    for j in range(half):
+        oa[:, cols(other + j)] = adjoint(other + j)
+
+    def local_backward(j, carry, base, kgl, vgl):
         h = base + j
-        kl[:, cols(j)] = k[:, cols(h)] * last_col[...]
-        vl[:, cols(j)] = v[:, cols(h)] * last_col[...]
+        kl[:, cols(h)] = k[:, cols(h)] * last_col[...]
+        vl[:, cols(h)] = v[:, cols(h)] * last_col[...]
         grads = oa[:, cols(h)]
         stepped = nt(grads, state[cols(h), :]) * first_col[...]
         for r in range(tiles):
@@ -472,60 +520,52 @@
         normed[:, cols(h)] = (gain[:, cols(h)] * att[:, cols(h)] * inv_col[...]).astype(BF16)
         return carry
 
-    own_half = functools.partial(
-        local_backward, base=mine, kgl=kgl_own, vgl=vgl_own, kl=kl_own, vl=vl_own
-    )
-    other_half = functools.partial(
-        local_backward, base=other, kgl=kgl_other, vgl=vgl_other, kl=kl_other, vl=vl_other
-    )
-    lax.fori_loop(0, half, own_half, 0, unroll=2)
+    lower = functools.partial(local_backward, base=0, kgl=kgl0, vgl=vgl0)
+    upper = functools.partial(local_backward, base=half, kgl=kgl1, vgl=vgl1)
+    lax.fori_loop(0, half, lower, 0, unroll=2)
     scan(1)
-    lax.fori_loop(0, half, other_half, 0, unroll=2)
+    lax.fori_loop(0, half, upper, 0, unroll=2)
 
     def enter_back(head, block):
-        back_own[cols(head), :] = block.astype(BF16)
-
-    descend(1, enter_back, lambda head: None)
-    last_products(kg_own, vg_own, kgl_own, vgl_own, kl_own, vl_own, back_own)
+        back_state[cols(mine + head), :] = block.astype(BF16)
+
+    descend(1, enter_back)
     stat_whole.wait_send()
-    for head in arrivals:
+    for d in reversed(row_offsets):
+        head = head_at(d)
         push_down(1, head).wait_recv()
-    back_other[...] = from_sib[1].astype(BF16)
+        back_state[cols(other + head), :] = from_sib[1, cols(head), :].astype(BF16)
     settle(1)
 
 
-def last_products(kg, vg, kgl, vgl, kl, vl, back_state):
-    for h in range(kg.shape[1] // DH):
-        at = slice(h * DH, (h + 1) * DH)
-        back = back_state[at, :]
-        kg[:, at] = (kgl[:, at] + nt(vl[:, at], back)).astype(BF16)
-        vg[:, at] = (vgl[:, at] + nn(kl[:, at], back)).astype(BF16)
-
-
 def finish(
-    normed, qg, kg_own, vg_own, kgl_other, vgl_other, kl_other, vl_other, back_other,
+    normed, qg, kgl0, kgl1, vgl0, vgl1, kl, vl, back_state,
     normed_hbm, qg_hbm, kg_hbm, vg_hbm,
-    kg_other, vg_other, out_sem,
+    kg, vg, out_sem,
 ):
-    core = lax.rem(lax.axis_index("ctx"), 2)
-    part = kg_other.shape[1]
-
-    def side(s):
-        return pl.ds(pl.multiple_of(s * part, part), part)
-
+    heads = kg.shape[1] // DH
     stores = [
         pltpu.make_async_copy(normed, normed_hbm, out_sem.at[0]),
         pltpu.make_async_copy(qg, qg_hbm, out_sem.at[1]),
-        pltpu.make_async_copy(kg_own, kg_hbm.at[:, side(core)], out_sem.at[2]),
-        pltpu.make_async_copy(vg_own, vg_hbm.at[:, side(core)], out_sem.at[3]),
     ]
     for copy in stores:
         copy.start()
-    last_products(kg_other, vg_other, kgl_other, vgl_other, kl_other, vl_other, back_other)
-    for i, (src, dst) in enumerate(((kg_other, kg_hbm), (vg_other, vg_hbm))):
-        copy = pltpu.make_async_copy(src, dst.at[:, side(1 - core)], out_sem.at[4 + i])
-        copy.start()
-        stores.append(copy)
+    parts = 2
+    per_part = heads // parts
+    for part, (kgl, vgl) in enumerate(((kgl0, vgl0), (kgl1, vgl1))):
+        for j in range(per_part):
+            here = slice(j * DH, (j + 1) * DH)
+            at = slice((part * per_part + j) * DH, (part * per_part + j + 1) * DH)
+            back = back_state[at, :]
+            kg[:, at] = (kgl[:, here] + nt(vl[:, at], back)).astype(BF16)
+            vg[:, at] = (vgl[:, here] + nn(kl[:, at], back)).astype(BF16)
+        done = slice(part * per_part * DH, (part + 1) * per_part * DH)
+        for i, (src, dst) in enumerate(((kg, kg_hbm), (vg, vg_hbm))):
+            copy = pltpu.make_async_copy(
+                src.at[:, done], dst.at[:, done], out_sem.at[2 + 2 * part + i]
+            )
+            copy.start()
+            stores.append(copy)
     for copy in stores:
         copy.wait()
 
@@ -548,7 +588,7 @@
         pltpu.VMEM((tokens, tokens), BF16),
         pltpu.VMEM((1, width), F32),
         pltpu.VMEM((1, tokens), jnp.int32),
-        pltpu.VMEM((heads * DH, tokens), BF16),
+        pltpu.VMEM((half * DH, tokens), BF16),
         *[pltpu.VMEM((tokens, DH), F32)] * 2,
         pltpu.VMEM((tokens, DH), BF16),
         *[pltpu.VMEM((tokens, DH), F32)] * 4,
@@ -558,12 +598,15 @@
         pltpu.VMEM((2, chips, rows + 8, DH), F32),
         *[pltpu.VMEM((2, half * DH, DH), F32)] * 4,
         pltpu.VMEM((heads * DH, DH), BF16),
-        *[pltpu.VMEM(half_grid, F32)] * 2,
-        *[pltpu.VMEM(half_grid, BF16)] * 2,
+        *[pltpu.VMEM((8, DH), F32)] * 3,
+        pltpu.VMEM((2, 2 * blocks, DH), F32),
+        pltpu.VMEM((2 * nhead, 2, 2 * blocks, DH), F32),
+        pltpu.VMEM((2, 2 * blocks, DH), F32),
+        *[pltpu.VMEM(half_grid, F32)] * 4,
+        pltpu.VMEM(half_grid, BF16),
+        pltpu.VMEM((half * DH, tokens), BF16),
         pltpu.VMEM((half * DH, DH), BF16),
-        *[pltpu.VMEM((8, DH), F32)] * 3,
-        pltpu.VMEM((2 * blocks, DH), F32),
-        pltpu.VMEM((nhead, 2 * blocks, DH), F32),
+        *[pltpu.VMEM((tokens, DH), F32)] * 4,
         dma((8,)),
         *[dma((2,))] * 2,
         dma((2, 2)),
@@ -572,6 +615,7 @@
         dma((2,)),
         dma((2, half)),
         dma((2,)),
+        *[dma((3,))] * 2,
     ]
     arrays = (
         query_rows, key_rows, value_rows, out_grad,
@@ -584,10 +628,9 @@
         functools.partial(kernel, nctx, nhead),
         out_shape=[
             *[jax.ShapeDtypeStruct(grid, BF16)] * 2,
-            *[jax.ShapeDtypeStruct(half_grid, BF16)] * 2,
-            *[jax.ShapeDtypeStruct(half_grid, F32)] * 2,
-            *[jax.ShapeDtypeStruct(half_grid, BF16)] * 2,
-            jax.ShapeDtypeStruct((half * DH, DH), BF16),
+            *[jax.ShapeDtypeStruct(half_grid, F32)] * 4,
+            *[jax.ShapeDtypeStruct(grid, BF16)] * 2,
+            jax.ShapeDtypeStruct((heads * DH, DH), BF16),
         ],
         in_specs=[in_hbm] * 6,
         out_specs=[in_vmem] * 9,
@@ -602,7 +645,7 @@
         out_shape=[jax.ShapeDtypeStruct(grid, BF16)] * 4,
         in_specs=[in_vmem] * 9,
         out_specs=[anywhere] * 4,
-        scratch_shapes=[*[pltpu.VMEM(half_grid, BF16)] * 2, dma((6,))],
+        scratch_shapes=[*[pltpu.VMEM(grid, BF16)] * 2, dma((6,))],
         compiler_params=pltpu.CompilerParams(vmem_limit_bytes=16 * 2**20),
         name="finish",
     )(*parts)

time: 48.8 us -> 47 us (0.963)
  Pallas kernels: 48.1 us -> 46.3 us
    pallas_call x1, Pallas kernels: 45.7 us -> 44.2 us  [body(): pl.pallas_call(functools.partial(kernel, nctx, nhead), out_shape=[*[jax.S...]
where the time goes in v4:
time: 47 us; the launch traced here: 46.9 us
  Pallas kernels  46.3 us (99%)
  between operations  0.64 us (1%)
    pallas_call x1, Pallas kernels, body(): pl.pallas_call(functools.partial(kernel, nctx, nhead), out_shape=[*[jax.S...  44.2 us
    pallas_call x1, Pallas kernels, body(): pl.pallas_call(finish, out_shape=[jax.ShapeDtypeStruct(grid, BF16)] * 4,...  2.06 us

profile of v4, /device:TPU:1, one launch (start us, length us, event | category | flops | bytes accessed | tf_op | source)
XLA Modules:
  0.0 46.9 jit_solution(5782308962273239682)
XLA Ops:
  0.6 44.2 %attend.1 = (bf16[512,1024]{1,0:T(8,128)(2,1)S(1)}, bf16[512,1024]{1,0:T(8,128)(2,1)S(1)}, f32[512,512]{1,0:T(8,128)S(1)}, f32[512,512]{1,0:T(8,128)S(1)}, f32[5...) custom-call(bf16[512,1024]{1,0:T(8,128)(2,1)} %q_hbm.1, ...), custom_call_target="tpu_custom_call" | custom-call | tf_op jit(solution)/shard_map/attend/pallas_call | solution.py:627
  44.8 2.1 %finish.1 = (bf16[512,1024]{1,0:T(8,128)(2,1)}, bf16[512,1024]{1,0:T(8,128)(2,1)}, bf16[512,1024]{1,0:T(8,128)(2,1)}, bf16[512,1024]{1,0:T(8,128)(2,1)}) custom-call(bf16[512,1024]{1,0:T(8,128)(2,1)S(1)} %get-tuple-element.13.normed, bf16[512,1024]{1,0:T(8,128)(2,1)S(1)} %get-tuple-element.14.qg, f32[512,512]{1,0:T(8,128)S(1)} %get-tuple-element.15.kgl0, ...), custom_call_target="tpu_custom_call" | custom-call | tf_op jit(solution)/shard_map/finish/pallas_call | solution.py:643

commit v5 on v4

--- a/solution.py
+++ b/solution.py
@@ -59,7 +59,7 @@
     first_col, last_col, inv_col, adj_col, sq_acc, gr_acc,
     piece, sib_piece, total, slices, scanned, landed, to_sib, from_sib, state,
     my_info, sib_info, chip_info, stat_out, stat_in, stat_sum,
-    qf_wide, qf_in, att_sib, scaled_sib, qf_sib, turned_sib, state_sib,
+    qf_wide, qf_in, att_sib, scaled_sib, qf_sib, turned_sib,
     sq_sib, gr_sib, inv_sib, adj_sib,
     in_sem, sib_sem, up_send, up_recv, a_send, a_recv, b_send, b_recv,
     down_send, down_recv, stat_sem, swap_send, swap_recv,
@@ -81,6 +81,7 @@
     mine, other = core * half, (1 - core) * half
     here_y, here_x = lax.div(chip, across), lax.rem(chip, across)
     row_offsets = sorted(range(along), key=lambda d: -min(d, along - d))
+    groups = [row_offsets[:1], row_offsets[1:-1], row_offsets[-1:]]
     column_offsets = sorted(range(across), key=lambda d: -min(d, across - d))
 
     def cols(h):
@@ -269,15 +270,19 @@
             up_heads(0, 0, half, heads).start()
             slices[0, chip] = total[chip]
 
-    def ascend_backward():
-        for head in range(half):
-            add_up(1, mine + head, 2 * chips + head * across)
-        for offset in chip_offsets:
-            i = chip_at(offset)
-            send_slice(
-                total.at[2 * chips + i, sent_rows(1)], slices.at[1, chip, sent_rows(1)],
-                a_send.at[1], a_recv.at[1], to_chip(i),
-            )
+    def ascend_backward(make):
+        for group in groups:
+            for d in group:
+                make(head_at(d))
+            for d in group:
+                add_up(1, mine + head_at(d), 2 * chips + head_at(d) * across)
+            for offset in chip_offsets:
+                if offset[0] in group:
+                    i = chip_at(offset)
+                    send_slice(
+                        total.at[2 * chips + i, sent_rows(1)], slices.at[1, chip, sent_rows(1)],
+                        a_send.at[1], a_recv.at[1], to_chip(i),
+                    )
         slices[1, chip] = total[2 * chips + chip]
 
     def scan(turn):
@@ -315,7 +320,7 @@
             )
         landed[turn, slot(chip), :] = scanned[turn, slot(chip), :]
 
-    def descend(turn, into):
+    def descend(turn, into, then):
         near_first, near_last, far_first, _ = orders(turn)
         next_to = equal(ids_of(near_last), ids_of(far_first))
         through = equal(ids_of(near_first), ids_of(far_first))
@@ -324,16 +329,19 @@
         own_sib = jnp.where(near, 0.0, next_to)
         sib_enter = jnp.where(near, through, 1.0)
         sib_own = jnp.where(near, next_to, 0.0)
-        for d in reversed(row_offsets):
-            head = head_at(d)
-            at = cols(head)
-            back_whole(turn, across - (d == 0), head).wait_recv()
-            to_sib[turn, at, :] = (
-                landed[turn, at, :] * sib_enter + piece[turn, cols(mine + head), :] * sib_own
-            )
-            push_down(turn, head).start()
-            beyond = sib_piece[turn, cols(mine + head), :]
-            into(head, landed[turn, at, :] * own_enter + beyond * own_sib)
+        for group in reversed(groups):
+            for d in group:
+                head = head_at(d)
+                at = cols(head)
+                back_whole(turn, across - (d == 0), head).wait_recv()
+                to_sib[turn, at, :] = (
+                    landed[turn, at, :] * sib_enter + piece[turn, cols(mine + head), :] * sib_own
+                )
+                push_down(turn, head).start()
+                beyond = sib_piece[turn, cols(mine + head), :]
+                into(head, landed[turn, at, :] * own_enter + beyond * own_sib)
+            for d in group:
+                then(head_at(d))
 
     sib_ids = to_sibling(my_info, sib_info, sib_sem.at[0], sib_sem.at[1])
 
@@ -419,22 +427,23 @@
     def enter(head, block):
         state[cols(mine + head), :] = block.astype(BF16)
 
-    descend(0, enter)
+    def attend(head):
+        h = mine + head
+        whole = att[:, cols(h)] + nn(qf[:, cols(h)], state[cols(h), :])
+        att[:, cols(h)] = whole
+        sq_acc[...] += whole * whole
+        gr_acc[...] += scaled[:, cols(h)] * whole
+        entering = to_sib[0, cols(head), :].astype(BF16)
+        whole = att_sib[:, cols(head)] + nn(qf_sib[:, cols(head)], entering)
+        att_sib[:, cols(head)] = whole
+        sq_sib[...] += whole * whole
+        gr_sib[...] += scaled_sib[:, cols(head)] * whole
+
     sq_acc[...] = jnp.zeros_like(sq_acc)
     gr_acc[...] = jnp.zeros_like(gr_acc)
     sq_sib[...] = jnp.zeros_like(sq_sib)
     gr_sib[...] = jnp.zeros_like(gr_sib)
-    state_sib[...] = to_sib[0].astype(BF16)
-    for j in range(half):
-        whole = att[:, cols(mine + j)] + nn(qf[:, cols(mine + j)], state[cols(mine + j), :])
-        att[:, cols(mine + j)] = whole
-        sq_acc[...] += whole * whole
-        gr_acc[...] += scaled[:, cols(mine + j)] * whole
-    for j in range(half):
-        whole = att_sib[:, cols(j)] + nn(qf_sib[:, cols(j)], state_sib[cols(j), :])
-        att_sib[:, cols(j)] = whole
-        sq_sib[...] += whole * whole
-        gr_sib[...] += scaled_sib[:, cols(j)] * whole
+    descend(0, enter, attend)
     for at, squares, grads in ((core, sq_acc, gr_acc), (1 - core, sq_sib, gr_sib)):
         square_sums, grad_sums = row_sums(squares[...]), row_sums(grads[...])
         for b in range(blocks):
@@ -488,16 +497,16 @@
     def adjoint(h):
         return (inv_col[...] * scaled[:, cols(h)] - att[:, cols(h)] * adj_col[...]).astype(BF16)
 
-    for j in range(half):
-        grads = adjoint(mine + j)
-        oa[:, cols(mine + j)] = grads
-        piece[1, cols(mine + j), :] = nn(qf_turned[cols(j), :], grads)
-    for j in range(half):
+    def back_pieces(head):
+        grads = adjoint(mine + head)
+        oa[:, cols(mine + head)] = grads
+        piece[1, cols(mine + head), :] = nn(qf_turned[cols(head), :], grads)
         grads = (
-            inv_sib[...] * scaled_sib[:, cols(j)] - att_sib[:, cols(j)] * adj_sib[...]
+            inv_sib[...] * scaled_sib[:, cols(head)] - att_sib[:, cols(head)] * adj_sib[...]
         ).astype(BF16)
-        sib_piece[1, cols(mine + j), :] = nn(turned_sib[cols(j), :], grads)
-    ascend_backward()
+        sib_piece[1, cols(mine + head), :] = nn(turned_sib[cols(head), :], grads)
+
+    ascend_backward(back_pieces)
     for j in range(half):
         oa[:, cols(other + j)] = adjoint(other + j)
 
@@ -529,7 +538,7 @@
     def enter_back(head, block):
         back_state[cols(mine + head), :] = block.astype(BF16)
 
-    descend(1, enter_back)
+    descend(1, enter_back, lambda head: None)
     stat_whole.wait_send()
     for d in reversed(row_offsets):
         head = head_at(d)
@@ -605,7 +614,6 @@
         *[pltpu.VMEM(half_grid, F32)] * 4,
         pltpu.VMEM(half_grid, BF16),
         pltpu.VMEM((half * DH, tokens), BF16),
-        pltpu.VMEM((half * DH, DH), BF16),
         *[pltpu.VMEM((tokens, DH), F32)] * 4,
         dma((8,)),
         *[dma((2,))] * 2,

time: 47 us -> 46.9 us (level)
  no operation moved by 1% of the time
where the time goes in v5:
time: 46.9 us; the launch traced here: 46.8 us
  Pallas kernels  46.1 us (98%)
  between operations  0.64 us (1%)
    pallas_call x1, Pallas kernels, body(): pl.pallas_call(functools.partial(kernel, nctx, nhead), out_shape=[*[jax.S...  44.1 us
    pallas_call x1, Pallas kernels, body(): pl.pallas_call(finish, out_shape=[jax.ShapeDtypeStruct(grid, BF16)] * 4,...  2.06 us

profile of v5, /device:TPU:1, one launch (start us, length us, event | category | flops | bytes accessed | tf_op | source)
XLA Modules:
  0.0 46.8 jit_solution(17882864490563518104)
XLA Ops:
  0.6 44.1 %attend.1 = (bf16[512,1024]{1,0:T(8,128)(2,1)S(1)}, bf16[512,1024]{1,0:T(8,128)(2,1)S(1)}, f32[512,512]{1,0:T(8,128)S(1)}, f32[512,512]{1,0:T(8,128)S(1)}, f32[5...) custom-call(bf16[512,1024]{1,0:T(8,128)(2,1)} %q_hbm.1, ...), custom_call_target="tpu_custom_call" | custom-call | tf_op jit(solution)/shard_map/attend/pallas_call | solution.py:635
  44.7 2.1 %finish.1 = (bf16[512,1024]{1,0:T(8,128)(2,1)}, bf16[512,1024]{1,0:T(8,128)(2,1)}, bf16[512,1024]{1,0:T(8,128)(2,1)}, bf16[512,1024]{1,0:T(8,128)(2,1)}) custom-call(bf16[512,1024]{1,0:T(8,128)(2,1)S(1)} %get-tuple-element.13.normed, bf16[512,1024]{1,0:T(8,128)(2,1)S(1)} %get-tuple-element.14.qg, f32[512,512]{1,0:T(8,128)S(1)} %get-tuple-element.15.kgl0, ...), custom_call_target="tpu_custom_call" | custom-call | tf_op jit(solution)/shard_map/finish/pallas_call | solution.py:651

commit v6 on v5

--- a/solution.py
+++ b/solution.py
@@ -48,7 +48,12 @@
         return min(dy, along - dy) + min(dx, across - dx)
 
     offsets = [(dy, dx) for dy in range(along) for dx in range(across) if dy + dx > 0]
-    return sorted(offsets, key=hops, reverse=True)
+    ordered = []
+    for dy, dx in sorted(offsets, key=hops, reverse=True):
+        for offset in ((dy, dx), (-dy % along, -dx % across)):
+            if offset not in ordered:
+                ordered.append(offset)
+    return ordered
 
 
 def kernel(
@@ -61,7 +66,7 @@
     my_info, sib_info, chip_info, stat_out, stat_in, stat_sum,
     qf_wide, qf_in, att_sib, scaled_sib, qf_sib, turned_sib,
     sq_sib, gr_sib, inv_sib, adj_sib,
-    in_sem, sib_sem, up_send, up_recv, a_send, a_recv, b_send, b_recv,
+    in_sem, sib_sem, up_sem, go_sem, a_send, a_recv, b_send, b_recv,
     down_send, down_recv, stat_sem, swap_send, swap_recv,
 ):
     tokens, width = q.shape
@@ -157,12 +162,9 @@
             device_id_type=MESH,
         )
 
-    def up_heads(turn, g, first, last):
-        at = slice(first * DH, last * DH)
-        return to_sibling(
-            piece.at[turn, at, :], sib_piece.at[turn, at, :],
-            up_send.at[turn], up_recv.at[turn, g],
-        )
+    def up_half():
+        at = pl.ds(pl.multiple_of(other * DH, half * DH), half * DH)
+        return to_sibling(piece.at[0, at, :], sib_piece.at[0, at, :], up_sem.at[0], up_sem.at[1])
 
     def push_down(turn, head):
         return to_sibling(
@@ -224,83 +226,76 @@
     def ascend_forward():
         for copy in first_loads:
             copy.wait()
+        for j in range(half):
+            make_piece(other + j)
 
         @pl.when(core == 1)
         def _():
-            for h in range(half):
-                make_piece(h)
             pl.semaphore_wait(barrier, 1)
             sib_ids.start()
-            up_heads(0, 0, 0, half).start()
-            for copy in own_loads:
-                copy.wait()
-            for h in range(half, heads):
-                make_piece(h)
-            up_heads(0, 1, half, heads).start()
+            up_half().start()
+
+        for copy in own_loads:
+            copy.wait()
 
         @pl.when(core == 0)
         def _():
-            for copy in own_loads:
-                copy.wait()
-            for h in range(heads):
-                make_piece(h)
             sib_ids.wait_recv()
-            chip_info[0:2, :] = my_info[0:2, :]
-            chip_info[2:4, :] = sib_info[0:2, :]
-            up_heads(0, 0, 0, half).wait_recv()
-            for head in range(half):
-                add_up(0, head, head * across)
-            up_heads(0, 1, half, heads).wait_recv()
-            for head in range(half, heads):
-                add_up(0, head, head * across)
-            for i in range(2 * chips):
-                total[i, rows : rows + 8, :] = chip_info[...]
+            sib_ids.start()
+            up_half().start()
+
+        for j in range(half):
+            make_piece(mine + j)
+
+        @pl.when(core == 1)
+        def _():
+            sib_ids.wait_recv()
+
+        near = is_near(0)
+        for at in range(2):
+            here, there = my_info[at : at + 1, :], sib_info[at : at + 1, :]
+            chip_info[at : at + 1, :] = jnp.where(near, here, there)
+            chip_info[at + 2 : at + 3, :] = jnp.where(near, there, here)
+        for i in range(chips):
+            total[i, rows : rows + 8, :] = chip_info[...]
+        up_half().wait_recv()
+        for head in range(half):
+            add_up(0, mine + head, head * across)
+
+        @pl.when(core == 0)
+        def _():
             pl.semaphore_wait(barrier, 1 + 2 * (chips - 1) + 2 * (nhead - 1))
-            for offset in chip_offsets:
-                i = chip_at(offset)
-                for a in range(2):
-                    send_slice(
-                        total.at[a * chips + i], slices.at[0, chip],
-                        a_send.at[0], a_recv.at[0], {"ctx": 2 * i + a},
-                    )
+            pl.semaphore_signal(go_sem, inc=1, device_id={"ctx": sibling}, device_id_type=MESH)
+
+        @pl.when(core == 1)
+        def _():
+            pl.semaphore_wait(go_sem, 1)
+
+        for offset in chip_offsets:
+            i = chip_at(offset)
             send_slice(
-                total.at[chips + chip], slices.at[0, chip],
-                a_send.at[0], a_recv.at[0], {"ctx": sibling},
+                total.at[i], slices.at[0, chip], a_send.at[0], a_recv.at[0], to_chip(i)
             )
-            up_heads(0, 0, half, heads).start()
-            slices[0, chip] = total[chip]
+        slices[0, chip] = total[chip]
 
     def ascend_backward(make):
         for group in groups:
             for d in group:
                 make(head_at(d))
             for d in group:
-                add_up(1, mine + head_at(d), 2 * chips + head_at(d) * across)
+                add_up(1, mine + head_at(d), chips + head_at(d) * across)
             for offset in chip_offsets:
                 if offset[0] in group:
                     i = chip_at(offset)
                     send_slice(
-                        total.at[2 * chips + i, sent_rows(1)], slices.at[1, chip, sent_rows(1)],
+                        total.at[chips + i, sent_rows(1)], slices.at[1, chip, sent_rows(1)],
                         a_send.at[1], a_recv.at[1], to_chip(i),
                     )
-        slices[1, chip] = total[2 * chips + chip]
+        slices[1, chip] = total[chips + chip]
 
     def scan(turn):
         near_first, _, _, far_last = orders(turn)
-        if turn == 0:
-
-            @pl.when(core == 0)
-            def _():
-                slices_whole(0, chips - 1).wait_recv()
-
-            @pl.when(core == 1)
-            def _():
-                slices_whole(0, chips).wait_recv()
-                up_heads(0, 0, half, heads).wait_recv()
-                chip_info[...] = slices[0, chip, rows : rows + 8, :]
-
-        else:
-            slices_whole(1, chips - 1).wait_recv()
+        slices_whole(turn, chips - 1).wait_recv()
         running = jnp.zeros((rows, DH), F32)
         before = jnp.full((1, DH), -1.0, F32)
         for j in range(chips):
@@ -351,22 +346,12 @@
         )
         whole.wait_send()
         back_whole(turn, chips - 1, 0).wait_send()
+        slices_whole(turn, chips - 1).wait_send()
         if turn == 0:
-
-            @pl.when(core == 0)
-            def _():
-                up_heads(0, 0, half, heads).wait_send()
-                slices_whole(0, 2 * chips - 1).wait_send()
-
-            @pl.when(core == 1)
-            def _():
-                up_heads(0, 0, 0, heads).wait_send()
-                sib_ids.wait_send()
-
+            up_half().wait_send()
+            sib_ids.wait_send()
             for n in range(3):
                 swap(n).wait_send()
-        else:
-            slices_whole(1, chips - 1).wait_send()
 
     def make_piece(h):
         piece[0, cols(h), :] = tn(k[:, cols(h)] * last_col[...], v[:, cols(h)])
@@ -603,7 +588,7 @@
         *[pltpu.VMEM((tokens, DH), F32)] * 4,
         pltpu.VMEM((2, heads * DH, DH), F32),
         pltpu.VMEM((2, heads * DH, DH), F32),
-        pltpu.VMEM((3 * chips, rows + 8, DH), F32),
+        pltpu.VMEM((2 * chips, rows + 8, DH), F32),
         pltpu.VMEM((2, chips, rows + 8, DH), F32),
         *[pltpu.VMEM((2, half * DH, DH), F32)] * 4,
         pltpu.VMEM((heads * DH, DH), BF16),
@@ -617,7 +602,7 @@
         *[pltpu.VMEM((tokens, DH), F32)] * 4,
         dma((8,)),
         *[dma((2,))] * 2,
-        dma((2, 2)),
+        pltpu.SemaphoreType.REGULAR,
         *[dma((2,))] * 3,
         dma((2, half)),
         dma((2,)),

time: 46.9 us -> 46.4 us (0.989)
  Pallas kernels: 46.1 us -> 45.6 us
    pallas_call x1, Pallas kernels: 44.1 us -> 43.6 us  [body(): pl.pallas_call(functools.partial(kernel, nctx, nhead), out_shape=[*[jax.S...]
where the time goes in v6:
time: 46.4 us; the launch traced here: 46.3 us
  Pallas kernels  45.6 us (98%)
  between operations  0.64 us (1%)
    pallas_call x1, Pallas kernels, body(): pl.pallas_call(functools.partial(kernel, nctx, nhead), out_shape=[*[jax.S...  43.6 us
    pallas_call x1, Pallas kernels, body(): pl.pallas_call(finish, out_shape=[jax.ShapeDtypeStruct(grid, BF16)] * 4,...  2.06 us

profile of v6, /device:TPU:1, one launch (start us, length us, event | category | flops | bytes accessed | tf_op | source)
XLA Modules:
  0.0 46.3 jit_solution(8213302498153522358)
XLA Ops:
  0.6 43.6 %attend.1 = (bf16[512,1024]{1,0:T(8,128)(2,1)S(1)}, bf16[512,1024]{1,0:T(8,128)(2,1)S(1)}, f32[512,512]{1,0:T(8,128)S(1)}, f32[512,512]{1,0:T(8,128)S(1)}, f32[5...) custom-call(bf16[512,1024]{1,0:T(8,128)(2,1)} %q_hbm.1, ...), custom_call_target="tpu_custom_call" | custom-call | tf_op jit(solution)/shard_map/attend/pallas_call | solution.py:620
  44.2 2.1 %finish.1 = (bf16[512,1024]{1,0:T(8,128)(2,1)}, bf16[512,1024]{1,0:T(8,128)(2,1)}, bf16[512,1024]{1,0:T(8,128)(2,1)}, bf16[512,1024]{1,0:T(8,128)(2,1)}) custom-call(bf16[512,1024]{1,0:T(8,128)(2,1)S(1)} %get-tuple-element.13.normed, bf16[512,1024]{1,0:T(8,128)(2,1)S(1)} %get-tuple-element.14.qg, f32[512,512]{1,0:T(8,128)S(1)} %get-tuple-element.15.kgl0, ...), custom_call_target="tpu_custom_call" | custom-call | tf_op jit(solution)/shard_map/finish/pallas_call | solution.py:636

commit v7 on v6

--- a/solution.py
+++ b/solution.py
@@ -544,20 +544,18 @@
     ]
     for copy in stores:
         copy.start()
-    parts = 2
-    per_part = heads // parts
-    for part, (kgl, vgl) in enumerate(((kgl0, vgl0), (kgl1, vgl1))):
-        for j in range(per_part):
-            here = slice(j * DH, (j + 1) * DH)
-            at = slice((part * per_part + j) * DH, (part * per_part + j + 1) * DH)
+    part = 2
+    for first in range(0, heads, part):
+        kgl, vgl = (kgl0, vgl0) if first < heads // 2 else (kgl1, vgl1)
+        for h in range(first, first + part):
+            j = h % (heads // 2)
+            here, at = slice(j * DH, (j + 1) * DH), slice(h * DH, (h + 1) * DH)
             back = back_state[at, :]
             kg[:, at] = (kgl[:, here] + nt(vl[:, at], back)).astype(BF16)
             vg[:, at] = (vgl[:, here] + nn(kl[:, at], back)).astype(BF16)
-        done = slice(part * per_part * DH, (part + 1) * per_part * DH)
+        done = slice(first * DH, (first + part) * DH)
         for i, (src, dst) in enumerate(((kg, kg_hbm), (vg, vg_hbm))):
-            copy = pltpu.make_async_copy(
-                src.at[:, done], dst.at[:, done], out_sem.at[2 + 2 * part + i]
-            )
+            copy = pltpu.make_async_copy(src.at[:, done], dst.at[:, done], out_sem.at[2 + first + i])
             copy.start()
             stores.append(copy)
     for copy in stores:
@@ -638,7 +636,7 @@
         out_shape=[jax.ShapeDtypeStruct(grid, BF16)] * 4,
         in_specs=[in_vmem] * 9,
         out_specs=[anywhere] * 4,
-        scratch_shapes=[*[pltpu.VMEM(grid, BF16)] * 2, dma((6,))],
+        scratch_shapes=[*[pltpu.VMEM(grid, BF16)] * 2, dma((2 + heads,))],
         compiler_params=pltpu.CompilerParams(vmem_limit_bytes=16 * 2**20),
         name="finish",
     )(*parts)

time: 46.4 us -> 46.4 us (level)
  no operation moved by 1% of the time
where the time goes in v7:
time: 46.4 us; the launch traced here: 46.3 us
  Pallas kernels  45.7 us (98%)
  between operations  0.64 us (1%)
    pallas_call x1, Pallas kernels, body(): pl.pallas_call(functools.partial(kernel, nctx, nhead), out_shape=[*[jax.S...  43.6 us
    pallas_call x1, Pallas kernels, body(): pl.pallas_call(finish, out_shape=[jax.ShapeDtypeStruct(grid, BF16)] * 4,...  2.09 us

profile of v7, /device:TPU:1, one launch (start us, length us, event | category | flops | bytes accessed | tf_op | source)
XLA Modules:
  0.0 46.3 jit_solution(816174802214840101)
XLA Ops:
  0.6 43.6 %attend.1 = (bf16[512,1024]{1,0:T(8,128)(2,1)S(1)}, bf16[512,1024]{1,0:T(8,128)(2,1)S(1)}, f32[512,512]{1,0:T(8,128)S(1)}, f32[512,512]{1,0:T(8,128)S(1)}, f32[5...) custom-call(bf16[512,1024]{1,0:T(8,128)(2,1)} %q_hbm.1, ...), custom_call_target="tpu_custom_call" | custom-call | tf_op jit(solution)/shard_map/attend/pallas_call | solution.py:618
  44.2 2.1 %finish.1 = (bf16[512,1024]{1,0:T(8,128)(2,1)}, bf16[512,1024]{1,0:T(8,128)(2,1)}, bf16[512,1024]{1,0:T(8,128)(2,1)}, bf16[512,1024]{1,0:T(8,128)(2,1)}) custom-call(bf16[512,1024]{1,0:T(8,128)(2,1)S(1)} %get-tuple-element.13.normed, bf16[512,1024]{1,0:T(8,128)(2,1)S(1)} %get-tuple-element.14.qg, f32[512,512]{1,0:T(8,128)S(1)} %get-tuple-element.15.kgl0, ...), custom_call_target="tpu_custom_call" | custom-call | tf_op jit(solution)/shard_map/finish/pallas_call | solution.py:634
